TPU v7x, 512 devices: a whole 4x4x16 slice. The times are simulated.
512 devices in a mesh: prow: 32 (over y, z_lo, core), pcol: 16 (over z_hi, x).
Axes of the slice: x: 4, y: 4, z: 16 (z_hi: 4, z_lo: 4; z = z_hi * 4 + z_lo), core: 2. Of those that a mesh axis runs over, the one named last changes fastest.
Arguments:
- ancestor_inverse: bfloat16 [16384, 16384], P('prow', 'pcol'), may hold values from -6 to 6
- factor_panel: bfloat16 [16384, 2048], P('prow', 'pcol'), may hold values from -0.046875 to 0.046875
- pattern: int32 [128, 16], replicated, may hold values 0 or 1
- diagonal_term: float32 [2048, 128], P('pcol'), may hold values from -6 to 6
Outputs:
- offdiag_inverse: bfloat16 [16384, 2048], P('prow', 'pcol')
- diag_inverse: float32 [2048, 128], P('pcol')
All inputs are finite; a program needn't handle non-finite values.
Results may differ from a plain program's by a relative error of at most 0.0065.
Values may be sent and summed in bfloat16 or wider, within the bound.
No kernel may reach another device: no remote copies, remote signals or barrier semaphores. Data moves between devices by JAX's collectives and lax.ppermute only.
A program may use at most 64 MiB of HBM per device.

v0:
```python
import jax
import jax.numpy as jnp
from jax import lax
from jax.sharding import PartitionSpec as P

W = 128


def broadcast(block, axis, source):
    block = jnp.where(lax.axis_index(axis) == source, block, jnp.zeros_like(block))
    return lax.psum(block, axis)


def block_sums(left_rows, right_rows, count):
    left = left_rows.astype(jnp.float32).reshape(left_rows.shape[0], count, W)
    right = right_rows.reshape(right_rows.shape[0], count, W)
    return jnp.einsum("rka,rkb->kab", left, right, precision=lax.Precision.HIGHEST)


def on_device(ancestor_inverse, factor_panel, pattern, diagonal_term):
    row_count = lax.axis_size("prow")
    col_count = lax.axis_size("pcol")
    ratio = row_count // col_count
    row_index = lax.axis_index("prow")
    col_index = lax.axis_index("pcol")
    local_rows = factor_panel.shape[0]
    local_cols = factor_panel.shape[1]
    row_blocks = local_rows // W
    col_blocks = local_cols // W
    local_mask = lax.dynamic_slice(
        pattern, (row_index * row_blocks, col_index * col_blocks), (row_blocks, col_blocks)
    )
    expanded = jnp.repeat(jnp.repeat(local_mask, W, axis=0), W, axis=1)
    masked = factor_panel * expanded.astype(jnp.bfloat16)
    row_panel = lax.all_gather(masked, "pcol", axis=1, tiled=True)
    gathered = []
    for offset in range(ratio):
        gathered.append(broadcast(row_panel, "prow", ratio * col_index + offset))
    column_panel = jnp.concatenate(gathered, axis=0)
    full_term = None
    full_term = jnp.dot(ancestor_inverse, column_panel, preferred_element_type=jnp.float32)
    product = lax.psum_scatter(full_term, "pcol", scatter_dimension=1, tiled=True)
    offdiag_inverse = (-product * expanded.astype(jnp.float32)).astype(jnp.bfloat16)
    partial_blocks = block_sums(masked, product, col_blocks)
    blocks = lax.psum(partial_blocks.astype(jnp.bfloat16), "prow").astype(jnp.float32)
    diag_inverse = diagonal_term + blocks.reshape(local_cols, W)
    return (offdiag_inverse, diag_inverse)


def solution(mesh):
    in_specs = (P("prow", "pcol"), P("prow", "pcol"), P(), P("pcol", None))
    out_specs = (P("prow", "pcol"), P("pcol", None))
    return jax.shard_map(
        on_device, mesh=mesh, in_specs=in_specs, out_specs=out_specs, check_vma=False
    )
```

profile of v0, /device:TPU:1, one launch (start us, length us, event | category | flops | bytes accessed | tf_op | source)
XLA Modules:
  0.0 724.2 jit_solution(3833720428483293516)
XLA Ops:
  7.2 0.0 copy-start
  7.2 0.0 all-gather.2.cloned.1.call-start
  7.2 0.8 convert_bitcast_fusion
  8.1 0.1 broadcast_bitcast_fusion.1
  8.2 1.7 broadcast_multiply_fusion
  9.8 0.0 all-gather.2.cloned.1.call-update
  9.9 0.0 all-reduce.3.cloned.1.call-start
  9.9 106.3 %all-gather.2.cloned.1.call-done = bf16[512,2048]{1,0:T(8,128)(2,1)} async-done(((bf16[512,128]{1,0:T(8,128)(2,1)}), bf16[512,2048]{1,0:T(8,128)(2,1)}) %all-gather.2.cloned.1.call-update) | async-done | bytes 2097168 | tf_op jit(solution)/shard_map/all_gather | solution.py:35
  116.2 3.8 broadcast_select_fusion.1
  120.0 0.0 all-reduce.3.cloned.1.call-update
  120.0 0.0 reduce-scatter.2.cloned.1.call-start
  120.1 299.8 %all-reduce.3.cloned.1.call-done = (bf16[512,2048]{1,0:T(8,128)(2,1)}, bf16[512,2048]{1,0:T(8,128)(2,1)}) async-done(((bf16[512,2048]{1,0:T(8,128)(2,1)}, bf16[512,2048]{1,0:T(8,128)(2,1)}), (bf16[512,2048]{1,0:T(8,128)(2,1)}, bf16[512,2048]{1,0:T(8,128)(2,1)})) %all-reduce.3.cloned.1.call-update) | async-done | bytes 4194320 | tf_op jit(solution)/shard_map/psum | solution.py:11
  419.8 0.0 copy-done
  419.9 6.6 fusion.4
  426.4 0.0 copy-start.1
  426.4 0.0 copy-start.2
  426.4 0.0 reduce-scatter.2.cloned.1.call-update
  426.4 0.1 broadcast_bitcast_fusion
  426.5 156.9 %reduce-scatter.2.cloned.1.call-done = f32[512,128]{0,1:T(8,128)} async-done(((f32[512,2048]{0,1:T(8,128)}), f32[512,128]{0,1:T(8,128)}) %reduce-scatter.2.cloned.1.call-update) | async-done | bytes 262160 | tf_op jit(solution)/shard_map/reduce_scatter | solution.py:42
  583.4 0.0 copy-done.1
  583.4 1.3 convolution_convert_fusion
  584.7 130.7 %psum.23 = bf16[128,128]{1,0:T(8,128)(2,1)S(1)} all-reduce(bf16[128,128]{1,0:T(8,128)(2,1)S(1)} %convolution_convert_fusion), channel_id=1, replica_groups=mesh['prow'=32,'pcol'=16] {'prow'}, use_global_device_ids=true, to_apply=%region_3.4 | all-reduce | flops 16384 | bytes 65536 | tf_op jit(solution)/shard_map/psum | solution.py:45
  715.3 1.0 multiply_convert_fusion
  716.3 0.8 copy.6
  717.1 0.0 copy-done.2
  717.1 0.6 convert_add_fusion
Async XLA Ops:
  7.2 412.7 %copy-start = (bf16[512,1024]{1,0:T(8,128)(2,1)S(1)}, bf16[512,1024]{1,0:T(8,128)(2,1)}, u32[]{:S(2)}) copy-start(bf16[512,1024]{1,0:T(8,128)(2,1)} %param.4) | copy-start | bytes 3145732
  7.2 109.0 %all-gather.2.cloned.1.call-start = ((), (), s32[]{:S(2)}) async-start(), calls=%async_computation.1 | async-start | bytes 2228224 | tf_op jit(solution)/shard_map/all_gather | solution.py:35
  9.9 410.0 %all-reduce.3.cloned.1.call-start = ((), (), s32[]{:S(2)}) async-start(), calls=%async_computation.3 | async-start | bytes 8388608 | tf_op jit(solution)/shard_map/psum | solution.py:11
  120.0 463.4 %reduce-scatter.2.cloned.1.call-start = ((), (), s32[]{:S(2)}) async-start(), calls=%async_computation.2 | async-start | bytes 4456448 | tf_op jit(solution)/shard_map/reduce_scatter | solution.py:42
  426.4 157.0 %copy-start.1 = (bf16[512,128]{1,0:T(8,128)(2,1)S(1)}, bf16[512,128]{1,0:T(8,128)(2,1)}, u32[]{:S(2)}) copy-start(bf16[512,128]{1,0:T(8,128)(2,1)} %broadcast_multiply_fusion) | copy-start | bytes 393220
  426.4 290.6 %copy-start.2 = (f32[128,128]{1,0:T(8,128)S(1)}, f32[128,128]{1,0:T(8,128)}, u32[]{:S(2)}) copy-start(f32[128,128]{1,0:T(8,128)} %param.7) | copy-start | bytes 196612
Sparse Core Ops, SparseCore 0:
  11.6 104.5 all-gather.1
  120.1 299.6 all-reduce.2
  426.6 156.7 reduce-scatter.1
where the time goes:
time: 729 us; the launch traced here: 724 us
  waiting for transfers between devices  563 us (77%)
  blocking collectives  131 us (18%)
  between operations  13.8 us (2%)
  other arithmetic  7.95 us (1%)
  matrix products  7.82 us (1%)
    psum x1, waiting for transfers between devices, broadcast(): return lax.psum(block, axis)  300 us
    reduce_scatter x1, waiting for transfers between devices, on_device(): lax.psum_scatter(full_term, 'pcol', scatter_dimension=1, tiled=True)  157 us
    psum x1, blocking collectives, on_device(): lax.psum(partial_blocks.astype(jnp.bfloat16), 'prow').astype(jnp.float32)  131 us
    all_gather x1, waiting for transfers between devices, on_device(): row_panel = lax.all_gather(masked, 'pcol', axis=1, tiled=True)  106 us
  transfers between devices with their start and end apart: 3, of which 3 were waited for; matrix products, arithmetic and copies ran while one was open for 0% of the time, Pallas kernels for 0%

commit v1 on v0

v1 whole, which is shorter than its diff:
```python
import jax
import jax.numpy as jnp
from jax import lax
from jax.sharding import PartitionSpec as P

W = 128
BF = jnp.bfloat16
F32 = jnp.float32
PROW, PCOL = 32, 16


def groups(count, key):
    found = {}
    for i in range(count):
        found.setdefault(key(i), []).append(i)
    return list(found.values())


ZLO = groups(PROW, lambda r: (r // 8, r % 2))
Y = groups(PROW, lambda r: r % 8)
X = groups(PCOL, lambda c: c // 4)
ZHI = groups(PCOL, lambda c: c % 4)
SWAP = [(r, r ^ 1) for r in range(PROW)]


def target(r, c):
    z_hi, x = c // 4, c % 4
    core = z_hi // 2
    z_lo = 2 * (z_hi % 2) + r % 2
    return ((x * 4 + z_lo) * 2 + core) * PCOL + r // 2


SPREAD = [(r * PCOL + c, target(r, c)) for r in range(PROW) for c in range(PCOL)]


def gather(block, axis, members):
    count = len(members[0])
    copies = jnp.broadcast_to(block[None], (count,) + block.shape)
    return lax.all_to_all(copies, axis, 0, 0, axis_index_groups=members)


def on_device(ancestor_inverse, factor_panel, pattern, diagonal_term):
    row_index = lax.axis_index("prow")
    col_index = lax.axis_index("pcol")
    core = row_index % 2
    rows = factor_panel.shape[0]
    row_blocks = rows // W
    local_mask = lax.dynamic_slice(
        pattern, (row_index * row_blocks, col_index), (row_blocks, 1)
    )
    expanded = jnp.broadcast_to(local_mask[:, :, None], (row_blocks, W, W)).reshape(rows, W)
    masked = factor_panel * expanded.astype(BF)
    other_inverse = lax.ppermute(ancestor_inverse, "prow", SWAP)
    block = lax.ppermute(masked, ("prow", "pcol"), SPREAD)
    panel = gather(gather(block, "prow", ZLO), "prow", Y)
    panel = panel.reshape(8, 2 * rows, W)

    def times(inverse):
        out = jnp.einsum("rc,kcn->krn", inverse, panel, preferred_element_type=F32)
        return out.astype(BF).reshape(4, 2, 1, rows, W)

    partial = jnp.concatenate([times(ancestor_inverse), times(other_inverse)], axis=2)
    partial = lax.all_to_all(partial, "pcol", 0, 0, axis_index_groups=X)
    partial = jnp.sum(partial.astype(F32), axis=0).astype(BF)
    mine = partial[:, 0]
    theirs = lax.ppermute(partial[:, 1], "prow", SWAP)
    low = jnp.where(core == 0, mine, theirs)
    high = jnp.where(core == 0, theirs, mine)
    partial = jnp.concatenate([low, high], axis=0)
    partial = lax.all_to_all(partial, "pcol", 0, 0, axis_index_groups=ZHI)
    product = jnp.sum(partial.astype(F32), axis=0)
    offdiag = (-product * expanded.astype(F32)).astype(BF)
    sums = lax.dot_general(
        masked, product.astype(BF), (((0,), (0,)), ((), ())), preferred_element_type=F32
    )
    pieces = sums.astype(BF).reshape(PROW, W // PROW, W)
    pieces = lax.all_to_all(pieces, "prow", 0, 0)
    piece = jnp.sum(pieces.astype(F32), axis=0).astype(BF)
    copies = jnp.broadcast_to(piece[None], (PROW,) + piece.shape)
    blocks = lax.all_to_all(copies, "prow", 0, 0).reshape(W, W)
    return offdiag, diagonal_term + blocks.astype(F32)


def solution(mesh):
    in_specs = (P("prow", "pcol"), P("prow", "pcol"), P(), P("pcol", None))
    out_specs = (P("prow", "pcol"), P("pcol", None))
    return jax.shard_map(
        on_device, mesh=mesh, in_specs=in_specs, out_specs=out_specs, check_vma=False
    )
```

time: 729 us -> 187 us (0.26)
  waiting for transfers between devices: 563 us -> 52 us
  blocking collectives: 131 us -> 85.6 us
  starting transfers between devices: 0.12 us -> 36.1 us
  between operations: 13.8 us -> 0.78 us
    psum x1 -> x0, waiting for transfers between devices: 300 us -> none  [broadcast(): return lax.psum(block, axis)]
    reduce_scatter x1 -> x0, waiting for transfers between devices: 157 us -> none  [on_device(): lax.psum_scatter(full_term, 'pcol', scatter_dimension=1, tiled=True)]
    psum x1 -> x0, blocking collectives: 131 us -> none  [on_device(): lax.psum(partial_blocks.astype(jnp.bfloat16), 'prow').astype(jnp.float32)]
    all_gather x1 -> x0, waiting for transfers between devices: 106 us -> none  [on_device(): row_panel = lax.all_gather(masked, 'pcol', axis=1, tiled=True)]
    all_to_all x0 -> x3, blocking collectives: none -> 85.6 us  [the longest x1 34.5 us: on_device(): partial = lax.all_to_all(partial, 'pcol', 0, 0, axis_index_groups=ZHI)]
    all_to_all x0 -> x3, waiting for transfers between devices: none -> 35.7 us  [the longest x1 21.4 us: gather(): return lax.all_to_all(copies, axis, 0, 0, axis_index_groups=members)]
    all_to_all x0 -> x3, starting transfers between devices: none -> 21.9 us  [the longest x1 9.21 us: gather(): return lax.all_to_all(copies, axis, 0, 0, axis_index_groups=members)]
    ppermute x0 -> x3, waiting for transfers between devices: none -> 16.2 us  [the longest x1 15.1 us: on_device(): block = lax.ppermute(masked, ('prow', 'pcol'), SPREAD)]
  transfers between devices with their start and end apart: 3 -> 6, of which waited for: 3 -> 5; matrix products, arithmetic and copies ran while one was open for 0% -> 1% of each run, Pallas kernels for 0% -> 0%
where the time goes in v1:
time: 187 us; the launch traced here: 186 us
  blocking collectives  85.6 us (46%)
  waiting for transfers between devices  52 us (28%)
  starting transfers between devices  36.1 us (19%)
  matrix products  4.66 us (2%)
  other arithmetic  3.44 us (2%)
  local copies, waits for them, and re-layouts  3.36 us (2%)
    all_to_all x1, blocking collectives, on_device(): partial = lax.all_to_all(partial, 'pcol', 0, 0, axis_index_groups=ZHI)  34.5 us
    all_to_all x1, blocking collectives, on_device(): partial = lax.all_to_all(partial, 'pcol', 0, 0, axis_index_groups=X)  28.6 us
    all_to_all x1, blocking collectives, gather(): return lax.all_to_all(copies, axis, 0, 0, axis_index_groups=members)  22.5 us
    all_to_all x1, waiting for transfers between devices, gather(): return lax.all_to_all(copies, axis, 0, 0, axis_index_groups=members)  21.4 us
    ppermute x1, waiting for transfers between devices, on_device(): block = lax.ppermute(masked, ('prow', 'pcol'), SPREAD)  15.1 us
    all_to_all x1, starting transfers between devices, gather(): return lax.all_to_all(copies, axis, 0, 0, axis_index_groups=members)  9.21 us
    all_to_all x1, starting transfers between devices, on_device(): pieces = lax.all_to_all(pieces, 'prow', 0, 0)  8.61 us
    all_to_all x1, waiting for transfers between devices, on_device(): pieces = lax.all_to_all(pieces, 'prow', 0, 0)  7.45 us
  transfers between devices with their start and end apart: 6, of which 5 were waited for; matrix products, arithmetic and copies ran while one was open for 1% of the time, Pallas kernels for 0%

profile of v1, /device:TPU:1, one launch (start us, length us, event | category | flops | bytes accessed | tf_op | source)
XLA Modules:
  0.0 186.0 jit_solution(15417107431373960747)
XLA Ops:
  0.6 0.8 convert_bitcast_fusion
  1.4 0.1 broadcast_bitcast_fusion.1
  1.5 1.0 broadcast_multiply_fusion
  2.5 4.9 %collective-permute-start = (bf16[512,128]{1,0:T(8,128)(2,1)S(1)}, bf16[512,128]{1,0:T(8,128)(2,1)S(1)}, u32[]{:S(2)}, u32[]{:S(2)}) collective-permute-start(bf16[512,128]{1,0:T(8,128)(2,1)S(1)} %broadcast_multiply_fusion), channel_id=1, source_target_pairs={{0,0},{1,128},{2,256},{3,384},{4,64},{5,192},{6,320},{7,448},{8,16... | collective-permute-start | bytes 393224 | tf_op jit(solution)/shard_map/ppermute | solution.py:54
  7.5 15.1 %collective-permute-done = bf16[512,128]{1,0:T(8,128)(2,1)S(1)} collective-permute-done((bf16[512,128]{1,0:T(8,128)(2,1)S(1)}, bf16[512,128]{1,0:T(8,128)(2,1)S(1)}, u32[]{:S(2)}, u32[]{:S(2)}) %collective-permute-start) | collective-permute-done | bytes 131104 | tf_op jit(solution)/shard_map/ppermute | solution.py:54
  22.6 0.1 broadcast_in_dim.32
  22.6 22.5 %all_to_all.30 = bf16[4,512,128]{2,1,0:T(8,128)(2,1)S(1)} all-to-all(bf16[4,512,128]{2,1,0:T(8,128)(2,1)S(1)} %broadcast_in_dim.32), channel_id=1, replica_groups={{0,32,64,96},{16,48,80,112},{128,160,192,224},{144,176,208,240},{256,28..., dimensions={0} | all-to-all | bytes 1048576 | tf_op jit(solution)/shard_map/all_to_all | solution.py:39
  45.1 1.7 broadcast_in_dim.33
  46.9 0.0 copy-start.1
  46.9 9.2 %all-to-all-start.1 = ((bf16[4,4,512,128]{3,2,1,0:T(8,128)(2,1)}), bf16[4,4,512,128]{3,2,1,0:T(8,128)(2,1)S(1)}, u32[]{:S(2)}, u32[]{:S(2)}) async-start(bf16[4,4,512,128]{3,2,1,0:T(8,128)(2,1)} %broadcast_in_dim.33), calls=%async_computation.1 | async-start | bytes 4194304 | tf_op jit(solution)/shard_map/all_to_all | solution.py:39
  56.1 0.0 copy-done.1
  56.1 3.4 %collective-permute-start.1 = (bf16[512,1024]{1,0:T(8,128)(2,1)S(1)}, bf16[512,1024]{1,0:T(8,128)(2,1)}, u32[]{:S(2)}, u32[]{:S(2)}) collective-permute-start(bf16[512,1024]{1,0:T(8,128)(2,1)S(1)} %copy-done.1), channel_id=1, source_target_pairs={{0,16},{16,0},{32,48},{48,32},{64,80},{80,64},{96,112},{112,96},{1... | collective-permute-start | bytes 3145736 | tf_op jit(solution)/shard_map/ppermute | solution.py:53
  59.5 21.4 %all-to-all-done.1 = bf16[4,4,512,128]{3,2,1,0:T(8,128)(2,1)S(1)} async-done(((bf16[4,4,512,128]{3,2,1,0:T(8,128)(2,1)}), bf16[4,4,512,128]{3,2,1,0:T(8,128)(2,1)S(1)}, u32[]{:S(2)}, u32[]{:S(2)}) %all-to-all-start.1) | async-done | bytes 2097184 | tf_op jit(solution)/shard_map/all_to_all | solution.py:39
  81.0 1.3 convolution_convert_fusion.1
  82.3 0.0 collective-permute-done.1
  82.3 2.5 %convolution_convert_fusion = bf16[8,128,512]{2,1,0:T(8,128)(2,1)S(1)} fusion(bf16[8,1024,128]{2,1,0:T(8,128)(2,1)S(1)} %bitcast.40, bf16[512,1024]{1,0:T(8,128)(2,1)} %collective-permute-done.1), kind=kOutput, calls=%fused_computation.1 | convolution fusion | flops 1074266112 | bytes 4194304 | tf_op jit(solution)/shard_map/rc,kcn->krn/dot_general | solution.py:59
  84.8 0.2 pad_maximum_fusion
  85.0 28.6 %all_to_all.31 = bf16[4,2,2,512,128]{3,4,1,2,0:T(8,128)(2,1)S(1)} all-to-all(bf16[4,2,2,512,128]{3,4,1,2,0:T(8,128)(2,1)S(1)} %pad_maximum_fusion), channel_id=1, replica_groups={{0,1,2,3},{4,5,6,7},{8,9,10,11},{12,13,14,15},{16,17,18,19},{20,21,22,2..., dimensions={0} | all-to-all | bytes 4194304 | tf_op jit(solution)/shard_map/all_to_all | solution.py:63
  113.6 0.6 reduce_sum.33
  114.2 5.9 %collective-permute-start.2 = (bf16[2,512,128]{1,2,0:T(8,128)(2,1)S(1)}, bf16[2,512,128]{1,2,0:T(8,128)(2,1)S(1)}, u32[]{:S(2)}, u32[]{:S(2)}) collective-permute-start(bf16[2,512,128]{1,2,0:T(8,128)(2,1)S(1)} %slice_bitcast_fusion), channel_id=1, source_target_pairs={{0,16},{16,0},{32,48},{48,32},{64,80},{80,64},{96,112},{112,96},{1... | collective-permute-start | bytes 786440 | tf_op jit(solution)/shard_map/ppermute | solution.py:66
  120.2 1.1 collective-permute-done.2
  121.3 0.0 copy-start
  121.4 34.5 %all_to_all.32 = bf16[4,512,128]{1,2,0:T(8,128)(2,1)S(1)} all-to-all(bf16[4,512,128]{1,2,0:T(8,128)(2,1)S(1)} %pad_maximum_fusion.1), channel_id=1, replica_groups={{0,4,8,12},{1,5,9,13},{2,6,10,14},{3,7,11,15},{16,20,24,28},{17,21,25,2..., dimensions={0} | all-to-all | bytes 1048576 | tf_op jit(solution)/shard_map/all_to_all | solution.py:70
  155.9 0.1 convert_reduce_fusion
  156.0 0.8 convolution_convert_fusion.2
  156.8 8.6 %all-to-all-start.4 = ((bf16[32,4,128]{2,1,0:T(4,128)(2,1)}), bf16[32,4,128]{2,1,0:T(4,128)(2,1)S(1)}, u32[]{:S(2)}, u32[]{:S(2)}) async-start(bf16[32,4,128]{2,1,0:T(4,128)(2,1)} %bitcast.15), calls=%async_computation.4 | async-start | bytes 65536 | tf_op jit(solution)/shard_map/all_to_all | solution.py:77
  165.4 0.1 broadcast_bitcast_fusion
  165.5 7.4 %all-to-all-done.4 = bf16[32,4,128]{2,1,0:T(4,128)(2,1)S(1)} async-done(((bf16[32,4,128]{2,1,0:T(4,128)(2,1)}), bf16[32,4,128]{2,1,0:T(4,128)(2,1)S(1)}, u32[]{:S(2)}, u32[]{:S(2)}) %all-to-all-start.4) | async-done | bytes 32800 | tf_op jit(solution)/shard_map/all_to_all | solution.py:77
  173.0 0.6 broadcast_in_dim.36
  173.6 4.0 %all-to-all-start.5 = ((bf16[32,4,128]{2,1,0:T(4,128)(2,1)}), bf16[32,4,128]{2,1,0:T(4,128)(2,1)S(1)}, u32[]{:S(2)}, u32[]{:S(2)}) async-start(bf16[32,4,128]{2,1,0:T(4,128)(2,1)} %broadcast_in_dim.36), calls=%async_computation.5 | async-start | bytes 65536 | tf_op jit(solution)/shard_map/all_to_all | solution.py:80
  177.7 0.8 copy.18
  178.5 6.8 %all-to-all-done.5 = bf16[32,4,128]{2,1,0:T(4,128)(2,1)S(1)} async-done(((bf16[32,4,128]{2,1,0:T(4,128)(2,1)}), bf16[32,4,128]{2,1,0:T(4,128)(2,1)S(1)}, u32[]{:S(2)}, u32[]{:S(2)}) %all-to-all-start.5) | async-done | bytes 32800 | tf_op jit(solution)/shard_map/all_to_all | solution.py:80
  185.3 0.0 copy-done
  185.3 0.6 convert_add_fusion
  (5 shorter events, 0.2 us)
Async XLA Ops:
  2.5 20.0 %collective-permute-start = (bf16[512,128]{1,0:T(8,128)(2,1)S(1)}, bf16[512,128]{1,0:T(8,128)(2,1)S(1)}, u32[]{:S(2)}, u32[]{:S(2)}) collective-permute-start(bf16[512,128]{1,0:T(8,128)(2,1)S(1)} %broadcast_multiply_fusion), channel_id=1, source_target_pairs={{0,0},{1,128},{2,256},{3,384},{4,64},{5,192},{6,320},{7,448},{8,16... | collective-permute-start | bytes 393224 | tf_op jit(solution)/shard_map/ppermute | solution.py:54
  46.9 9.2 %copy-start.1 = (bf16[512,1024]{1,0:T(8,128)(2,1)S(1)}, bf16[512,1024]{1,0:T(8,128)(2,1)}, u32[]{:S(2)}) copy-start(bf16[512,1024]{1,0:T(8,128)(2,1)} %param.4) | copy-start | bytes 3145732
  46.9 34.1 %all-to-all-start.1 = ((bf16[4,4,512,128]{3,2,1,0:T(8,128)(2,1)}), bf16[4,4,512,128]{3,2,1,0:T(8,128)(2,1)S(1)}, u32[]{:S(2)}, u32[]{:S(2)}) async-start(bf16[4,4,512,128]{3,2,1,0:T(8,128)(2,1)} %broadcast_in_dim.33), calls=%async_computation.1 | async-start | bytes 4194304 | tf_op jit(solution)/shard_map/all_to_all | solution.py:39
  56.1 26.2 %collective-permute-start.1 = (bf16[512,1024]{1,0:T(8,128)(2,1)S(1)}, bf16[512,1024]{1,0:T(8,128)(2,1)}, u32[]{:S(2)}, u32[]{:S(2)}) collective-permute-start(bf16[512,1024]{1,0:T(8,128)(2,1)S(1)} %copy-done.1), channel_id=1, source_target_pairs={{0,16},{16,0},{32,48},{48,32},{64,80},{80,64},{96,112},{112,96},{1... | collective-permute-start | bytes 3145736 | tf_op jit(solution)/shard_map/ppermute | solution.py:53
  114.2 7.1 %collective-permute-start.2 = (bf16[2,512,128]{1,2,0:T(8,128)(2,1)S(1)}, bf16[2,512,128]{1,2,0:T(8,128)(2,1)S(1)}, u32[]{:S(2)}, u32[]{:S(2)}) collective-permute-start(bf16[2,512,128]{1,2,0:T(8,128)(2,1)S(1)} %slice_bitcast_fusion), channel_id=1, source_target_pairs={{0,16},{16,0},{32,48},{48,32},{64,80},{80,64},{96,112},{112,96},{1... | collective-permute-start | bytes 786440 | tf_op jit(solution)/shard_map/ppermute | solution.py:66
  121.3 64.0 %copy-start = (f32[128,128]{1,0:T(8,128)S(1)}, f32[128,128]{1,0:T(8,128)}, u32[]{:S(2)}) copy-start(f32[128,128]{1,0:T(8,128)} %param.7) | copy-start | bytes 196612
  156.8 16.1 %all-to-all-start.4 = ((bf16[32,4,128]{2,1,0:T(4,128)(2,1)}), bf16[32,4,128]{2,1,0:T(4,128)(2,1)S(1)}, u32[]{:S(2)}, u32[]{:S(2)}) async-start(bf16[32,4,128]{2,1,0:T(4,128)(2,1)} %bitcast.15), calls=%async_computation.4 | async-start | bytes 65536 | tf_op jit(solution)/shard_map/all_to_all | solution.py:77
  173.6 11.7 %all-to-all-start.5 = ((bf16[32,4,128]{2,1,0:T(4,128)(2,1)}), bf16[32,4,128]{2,1,0:T(4,128)(2,1)S(1)}, u32[]{:S(2)}, u32[]{:S(2)}) async-start(bf16[32,4,128]{2,1,0:T(4,128)(2,1)} %broadcast_in_dim.36), calls=%async_computation.5 | async-start | bytes 65536 | tf_op jit(solution)/shard_map/all_to_all | solution.py:80

commit v2 on v1

v2 whole, which is shorter than its diff:
```python
import jax
import jax.numpy as jnp
from jax import lax
from jax.experimental import pallas as pl
from jax.experimental.pallas import tpu as pltpu
from jax.sharding import PartitionSpec as P

W = 128
BF = jnp.bfloat16
F32 = jnp.float32
PROW, PCOL = 32, 16
BOTH = ("prow", "pcol")
TAIL = 1
COST = 18
VMEM_MB = 32


def groups(count, key):
    found = {}
    for i in range(count):
        found.setdefault(key(i), []).append(i)
    return list(found.values())


ZLO = groups(PROW, lambda r: (r // 8, r % 2))
Y = groups(PROW, lambda r: r % 8)
YC = groups(PROW, lambda r: r // 2 % 4)
ZC = groups(PROW, lambda r: r // 8)
X = groups(PCOL, lambda c: c // 4)
ZHI = groups(PCOL, lambda c: c % 4)


def place(y, z_lo, core, z_hi, x):
    return ((y * 4 + z_lo) * 2 + core) * PCOL + z_hi * 4 + x


def moves(to):
    pairs = []
    for device in range(PROW * PCOL):
        r, c = divmod(device, PCOL)
        pairs.append((device, place(*to(r // 8, r // 2 % 4, r % 2, c // 4, c % 4))))
    return pairs


def send(block, to):
    return lax.ppermute(block, BOTH, moves(to))


def spread(y, z_lo, core, z_hi, x):
    return z_lo, 2 * (z_hi % 2) + core, z_hi // 2, y, x


def swap(y, z_lo, core, z_hi, x):
    return y, z_lo, 1 - core, z_hi, x


def along_y(d):
    return lambda y, z_lo, core, z_hi, x: ((y + d) % 4, z_lo, core, z_hi, x)


def along_z_lo(d):
    return lambda y, z_lo, core, z_hi, x: (y, (z_lo + d) % 4, core, z_hi, x)


def along_x(d):
    return lambda y, z_lo, core, z_hi, x: (y, z_lo, core, z_hi, (x + d) % 4)


def home(s, t):
    return lambda y, z_lo, core, z_hi, x: (y, z_lo, (z_hi // 2) ^ s, 2 * core + ((z_hi % 2) ^ t), x)


def pick(stack, index):
    return lax.dynamic_index_in_dim(stack, index, 0, keepdims=False)


def gather(block, axis, members):
    count = len(members[0])
    copies = jnp.broadcast_to(block[None], (count,) + block.shape)
    return lax.all_to_all(copies, axis, 0, 0, axis_index_groups=members)


def times_kernel(swapped, panel, mine, other, first, second):
    tile = 256

    def product(part, rows):
        total = jnp.dot(part[0, rows], panel[0], preferred_element_type=F32)
        for d in range(1, 4):
            total += jnp.dot(part[d, rows], panel[d], preferred_element_type=F32)
        return total.astype(BF)

    for start in range(0, mine.shape[1], tile):
        rows = pl.ds(start, tile)
        ours = product(mine, rows)
        others = product(other, rows)

        @pl.when(swapped[0] == 0)
        def _():
            first[rows] = ours
            second[rows] = others

        @pl.when(swapped[0] != 0)
        def _():
            first[rows] = others
            second[rows] = ours


def times(swapped, mine, other, panel):
    count, rows, depth = mine.shape
    return pl.pallas_call(
        times_kernel,
        in_specs=[pl.BlockSpec(memory_space=pltpu.SMEM)] + [pl.BlockSpec(memory_space=pltpu.VMEM)] * 3,
        out_specs=[pl.BlockSpec(memory_space=pltpu.VMEM)] * 2,
        out_shape=[jax.ShapeDtypeStruct((rows, W), BF)] * 2,
        compiler_params=pltpu.CompilerParams(vmem_limit_bytes=VMEM_MB * 1024 * 1024),
        cost_estimate=pl.CostEstimate(
            flops=2 * 2 * count * rows * depth * W, bytes_accessed=COST * rows * depth, transcendentals=0
        ),
    )(swapped, panel, mine, other)


def on_device(ancestor_inverse, factor_panel, pattern, diagonal_term):
    row_index = lax.axis_index("prow")
    col_index = lax.axis_index("pcol")
    y, z_lo, core = row_index // 8, row_index // 2 % 4, row_index % 2
    z_hi, x = col_index // 4, col_index % 4
    rows = factor_panel.shape[0]
    row_blocks = rows // W
    local_mask = lax.dynamic_slice(
        pattern, (row_index * row_blocks, col_index), (row_blocks, 1)
    )
    expanded = jnp.broadcast_to(local_mask[:, :, None], (row_blocks, W, W)).reshape(rows, W)
    masked = factor_panel * expanded.astype(BF)
    mine = gather(ancestor_inverse, "pcol", X)
    block = send(masked, spread)
    near = jnp.stack([block] + [send(block, along_z_lo(d)) for d in range(1, 4)])
    near, mine = lax.optimization_barrier((near, mine))
    other = send(mine, swap)
    far = []
    for t in range(2):
        b = (z_hi % 2) ^ t
        both = jnp.stack([pick(near, (z_lo - 2 * b - j) % 4) for j in range(2)])
        far.append(gather(both, "prow", Y).reshape(4, 2 * rows, W))
    swapped = ((z_hi // 2) ^ core)[None]
    product = 0
    for t in range(2):
        pieces = times(swapped, mine, other, far[t])
        for s in range(2):
            product += send(pieces[s], home(s, t)).astype(F32)
    offdiag = (-product * expanded.astype(F32)).astype(BF)
    sums = lax.dot_general(
        masked, product.astype(BF), (((0,), (0,)), ((), ())), preferred_element_type=F32
    )
    if TAIL == 0:
        pieces = sums.astype(BF).reshape(PROW, W // PROW, W)
        pieces = lax.all_to_all(pieces, "prow", 0, 0)
        piece = jnp.sum(pieces.astype(F32), axis=0).astype(BF)
        blocks = gather(piece, "prow", [list(range(PROW))]).reshape(W, W).astype(F32)
    else:
        wide, narrow = ((YC, ZLO), (ZC, Y))[TAIL - 1]
        blocks = jnp.sum(gather(sums.astype(BF), "prow", wide).astype(F32), axis=0)
        blocks = jnp.sum(gather(blocks.astype(BF), "prow", narrow).astype(F32), axis=0)
    return offdiag, diagonal_term + blocks


def solution(mesh):
    in_specs = (P("prow", "pcol"), P("prow", "pcol"), P(), P("pcol", None))
    out_specs = (P("prow", "pcol"), P("pcol", None))
    return jax.shard_map(
        on_device, mesh=mesh, in_specs=in_specs, out_specs=out_specs, check_vma=False
    )
```

time: 187 us -> 163 us (0.87)
  blocking collectives: 85.6 us -> 16.4 us
  starting transfers between devices: 36.1 us -> 72.4 us
  Pallas kernels: 0 us -> 12 us
  matrix products: 4.66 us -> 0.23 us
  local copies, waits for them, and re-layouts: 3.36 us -> 7.03 us
    all_to_all x2 -> x0, blocking collectives: 63.1 us -> none  [the longest x1 34.5 us: on_device(): partial = lax.all_to_all(partial, 'pcol', 0, 0, axis_index_groups=ZHI)]
    ppermute x3 -> x9, starting transfers between devices: 14.3 us -> 56.2 us  [send(): return lax.ppermute(block, BOTH, moves(to))]
    ppermute x3 -> x9, waiting for transfers between devices: 16.2 us -> 31.4 us  [send(): return lax.ppermute(block, BOTH, moves(to))]
    all_to_all x2 -> x0, waiting for transfers between devices: 14.3 us -> none  [the longest x1 7.45 us: on_device(): pieces = lax.all_to_all(pieces, 'prow', 0, 0)]
    all_to_all x2 -> x0, starting transfers between devices: 12.7 us -> none  [the longest x1 8.61 us: on_device(): pieces = lax.all_to_all(pieces, 'prow', 0, 0)]
    pallas_call x0 -> x2, Pallas kernels: none -> 12 us  [times(): pl.pallas_call(times_kernel, in_specs=[pl.BlockSpec(memory_space=pltpu.SM...]
    all_to_all x1 -> x4, starting transfers between devices: 9.21 us -> 16.2 us  [gather(): return lax.all_to_all(copies, axis, 0, 0, axis_index_groups=members)]
    all_to_all x1, blocking collectives: 22.5 us -> 16.4 us  [gather(): return lax.all_to_all(copies, axis, 0, 0, axis_index_groups=members)]
  transfers between devices with their start and end apart: 6 -> 13, of which waited for: 5 -> 6; matrix products, arithmetic and copies ran while one was open for 1% -> 3% of each run, Pallas kernels for 0% -> 7%
where the time goes in v2:
time: 163 us; the launch traced here: 162 us
  starting transfers between devices  72.4 us (44%)
  waiting for transfers between devices  50.7 us (31%)
  blocking collectives  16.4 us (10%)
  Pallas kernels  12 us (7%)
  local copies, waits for them, and re-layouts  7.03 us (4%)
  other arithmetic  2.51 us (2%)
    ppermute x9, starting transfers between devices, send(): return lax.ppermute(block, BOTH, moves(to))  56.2 us
    ppermute x9, waiting for transfers between devices, send(): return lax.ppermute(block, BOTH, moves(to))  31.4 us
    all_to_all x4, waiting for transfers between devices, gather(): return lax.all_to_all(copies, axis, 0, 0, axis_index_groups=members)  19.2 us
    all_to_all x1, blocking collectives, gather(): return lax.all_to_all(copies, axis, 0, 0, axis_index_groups=members)  16.4 us
    all_to_all x4, starting transfers between devices, gather(): return lax.all_to_all(copies, axis, 0, 0, axis_index_groups=members)  16.2 us
    pallas_call x2, Pallas kernels, times(): pl.pallas_call(times_kernel, in_specs=[pl.BlockSpec(memory_space=pltpu.SM...  12 us
    broadcast_in_dim x5, local copies, waits for them, and re-layouts, gather(): copies = jnp.broadcast_to(block[None], (count,) + block.shape)  6.83 us
  transfers between devices with their start and end apart: 13, of which 6 were waited for; matrix products, arithmetic and copies ran while one was open for 3% of the time, Pallas kernels for 7%

profile of v2, /device:TPU:1, one launch (start us, length us, event | category | flops | bytes accessed | tf_op | source)
XLA Modules:
  0.0 162.3 jit_solution(12253824755031983013)
XLA Ops:
  0.6 3.7 %broadcast_in_dim.23 = bf16[4,512,1024]{2,1,0:T(8,128)(2,1)} broadcast(bf16[512,1024]{1,0:T(8,128)(2,1)} %param.4), dimensions={1,2} | broadcast | bytes 5242880 | tf_op jit(solution)/shard_map/broadcast_in_dim | solution.py:79
  4.4 0.0 copy-start
  4.4 5.0 %all-to-all-start = ((bf16[4,512,1024]{2,1,0:T(8,128)(2,1)}), bf16[4,512,1024]{2,1,0:T(8,128)(2,1)}, u32[]{:S(2)}, u32[]{:S(2)}) async-start(bf16[4,512,1024]{2,1,0:T(8,128)(2,1)} %broadcast_in_dim.23), calls=%async_computation | async-start | bytes 8388608 | tf_op jit(solution)/shard_map/all_to_all | solution.py:80
  9.4 0.8 convert_bitcast_fusion.1
  10.1 0.1 broadcast_bitcast_fusion.1
  10.2 0.0 copy-done
  10.2 0.1 broadcast_multiply_fusion
  10.4 4.9 %collective-permute-start = (bf16[512,128]{1,0:T(8,128)(2,1)S(1)}, bf16[512,128]{1,0:T(8,128)(2,1)S(1)}, u32[]{:S(2)}, u32[]{:S(2)}) collective-permute-start(bf16[512,128]{1,0:T(8,128)(2,1)S(1)} %broadcast_multiply_fusion), channel_id=1, source_target_pairs={{0,0},{1,1},{2,2},{3,3},{4,64},{5,65},{6,66},{7,67},{8,16},{9,17},... | collective-permute-start | bytes 393224 | tf_op jit(solution)/shard_map/ppermute | solution.py:46
  15.3 15.1 %collective-permute-done = bf16[512,128]{1,0:T(8,128)(2,1)S(1)} collective-permute-done((bf16[512,128]{1,0:T(8,128)(2,1)S(1)}, bf16[512,128]{1,0:T(8,128)(2,1)S(1)}, u32[]{:S(2)}, u32[]{:S(2)}) %collective-permute-start) | collective-permute-done | bytes 131104 | tf_op jit(solution)/shard_map/ppermute | solution.py:46
  30.4 9.7 %collective-permute-start.3 = (bf16[512,128]{1,0:T(8,128)(2,1)S(1)}, bf16[512,128]{1,0:T(8,128)(2,1)S(1)}, u32[]{:S(2)}, u32[]{:S(2)}) collective-permute-start(bf16[512,128]{1,0:T(8,128)(2,1)S(1)} %collective-permute-done), channel_id=1, source_target_pairs={{0,96},{1,97},{2,98},{3,99},{4,100},{5,101},{6,102},{7,103},{8,104... | collective-permute-start | bytes 393224 | tf_op jit(solution)/shard_map/ppermute | solution.py:46
  40.2 1.9 %collective-permute-start.2 = (bf16[512,128]{1,0:T(8,128)(2,1)S(1)}, bf16[512,128]{1,0:T(8,128)(2,1)S(1)}, u32[]{:S(2)}, u32[]{:S(2)}) collective-permute-start(bf16[512,128]{1,0:T(8,128)(2,1)S(1)} %collective-permute-done), channel_id=1, source_target_pairs={{0,64},{1,65},{2,66},{3,67},{4,68},{5,69},{6,70},{7,71},{8,72},{9,... | collective-permute-start | bytes 393224 | tf_op jit(solution)/shard_map/ppermute | solution.py:46
  42.1 3.3 %collective-permute-start.1 = (bf16[512,128]{1,0:T(8,128)(2,1)S(1)}, bf16[512,128]{1,0:T(8,128)(2,1)S(1)}, u32[]{:S(2)}, u32[]{:S(2)}) collective-permute-start(bf16[512,128]{1,0:T(8,128)(2,1)S(1)} %collective-permute-done), channel_id=1, source_target_pairs={{0,32},{1,33},{2,34},{3,35},{4,36},{5,37},{6,38},{7,39},{8,40},{9,... | collective-permute-start | bytes 393224 | tf_op jit(solution)/shard_map/ppermute | solution.py:46
  45.4 0.0 collective-permute-done.3
  45.4 6.6 %collective-permute-done.2 = bf16[512,128]{1,0:T(8,128)(2,1)S(1)} collective-permute-done((bf16[512,128]{1,0:T(8,128)(2,1)S(1)}, bf16[512,128]{1,0:T(8,128)(2,1)S(1)}, u32[]{:S(2)}, u32[]{:S(2)}) %collective-permute-start.2) | collective-permute-done | bytes 131104 | tf_op jit(solution)/shard_map/ppermute | solution.py:46
  52.1 0.0 collective-permute-done.1
  52.1 0.1 pad_maximum_fusion
  52.1 0.4 all-to-all-done.mine
  52.6 9.1 %collective-permute-start.4 = (bf16[4,512,1024]{2,1,0:T(8,128)(2,1)}, bf16[4,512,1024]{2,1,0:T(8,128)(2,1)}, u32[]{:S(2)}, u32[]{:S(2)}) collective-permute-start(bf16[4,512,1024]{2,1,0:T(8,128)(2,1)} %all-to-all-done.mine), channel_id=1, source_target_pairs={{0,16},{1,17},{2,18},{3,19},{4,20},{5,21},{6,22},{7,23},{8,24},{9,... | collective-permute-start | bytes 12582920 | tf_op jit(solution)/shard_map/ppermute | solution.py:46
  61.9 1.2 broadcast_in_dim.50
  63.1 4.4 %all-to-all-start.2 = ((bf16[4,2,512,128]{3,2,1,0:T(8,128)(2,1)}), bf16[4,2,512,128]{3,2,1,0:T(8,128)(2,1)S(1)}, u32[]{:S(2)}, u32[]{:S(2)}) async-start(bf16[4,2,512,128]{3,2,1,0:T(8,128)(2,1)} %broadcast_in_dim.50), calls=%async_computation.2 | async-start | bytes 2097152 | tf_op jit(solution)/shard_map/all_to_all | solution.py:80
  67.6 14.9 %all-to-all-done.2 = bf16[4,2,512,128]{3,2,1,0:T(8,128)(2,1)S(1)} async-done(((bf16[4,2,512,128]{3,2,1,0:T(8,128)(2,1)}), bf16[4,2,512,128]{3,2,1,0:T(8,128)(2,1)S(1)}, u32[]{:S(2)}, u32[]{:S(2)}) %all-to-all-start.2) | async-done | bytes 1048608 | tf_op jit(solution)/shard_map/all_to_all | solution.py:80
  82.5 1.2 broadcast_in_dim.24
  83.6 3.5 %all-to-all-start.1 = ((bf16[4,2,512,128]{3,2,1,0:T(8,128)(2,1)}), bf16[4,2,512,128]{3,2,1,0:T(8,128)(2,1)S(1)}, u32[]{:S(2)}, u32[]{:S(2)}) async-start(bf16[4,2,512,128]{3,2,1,0:T(8,128)(2,1)} %broadcast_in_dim.24), calls=%async_computation.1 | async-start | bytes 2097152 | tf_op jit(solution)/shard_map/all_to_all | solution.py:80
  87.2 0.0 collective-permute-done.4.other
  87.2 6.0 %shard_map.60 = (bf16[512,128]{1,0:T(8,128)(2,1)S(1)}, bf16[512,128]{1,0:T(8,128)(2,1)S(1)}) custom-call(s32[1]{0:T(128)} %bitcast.swapped, bf16[4,1024,128]{2,1,0:T(8,128)(2,1)S(1)} %bitcast.17, bf16[4,512,1024]{2,1,0:T(8,128)(2,1)} %all-to-all-done.mine, bf16[4,512,1024]{2,1,0:T(8,128)(2,1)} %collective-permute-done.4.other), custom_call_target="tpu_custom_call" | custom-call | flops 1073741824 | bytes 9437184 | tf_op jit(solution)/shard_map/pallas_call | solution.py:110
  93.2 13.5 %collective-permute-start.7 = (bf16[512,128]{1,0:T(8,128)(2,1)S(1)}, bf16[512,128]{1,0:T(8,128)(2,1)S(1)}, u32[]{:S(2)}, u32[]{:S(2)}) collective-permute-start(bf16[512,128]{1,0:T(8,128)(2,1)S(1)} %get-tuple-element.12), channel_id=1, source_target_pairs={{0,4},{1,5},{2,6},{3,7},{4,0},{5,1},{6,2},{7,3},{8,20},{9,21},{10,... | collective-permute-start | bytes 393224 | tf_op jit(solution)/shard_map/ppermute | solution.py:46
  106.7 4.2 %collective-permute-start.8 = (bf16[512,128]{1,0:T(8,128)(2,1)S(1)}, bf16[512,128]{1,0:T(8,128)(2,1)S(1)}, u32[]{:S(2)}, u32[]{:S(2)}) collective-permute-start(bf16[512,128]{1,0:T(8,128)(2,1)S(1)} %get-tuple-element.13), channel_id=1, source_target_pairs={{0,20},{1,21},{2,22},{3,23},{4,16},{5,17},{6,18},{7,19},{8,4},{9,5... | collective-permute-start | bytes 393224 | tf_op jit(solution)/shard_map/ppermute | solution.py:46
  110.8 0.0 all-to-all-done.1
  110.9 0.0 copy-start.1
  110.9 6.0 %shard_map.59 = (bf16[512,128]{1,0:T(8,128)(2,1)S(1)}, bf16[512,128]{1,0:T(8,128)(2,1)S(1)}) custom-call(s32[1]{0:T(128)} %bitcast.swapped, bf16[4,1024,128]{2,1,0:T(8,128)(2,1)S(1)} %bitcast.16, bf16[4,512,1024]{2,1,0:T(8,128)(2,1)} %all-to-all-done.mine, bf16[4,512,1024]{2,1,0:T(8,128)(2,1)} %collective-permute-done.4.other), custom_call_target="tpu_custom_call" | custom-call | flops 1073741824 | bytes 9437184 | tf_op jit(solution)/shard_map/pallas_call | solution.py:110
  116.9 7.6 %collective-permute-start.5 = (bf16[512,128]{1,0:T(8,128)(2,1)S(1)}, bf16[512,128]{1,0:T(8,128)(2,1)S(1)}, u32[]{:S(2)}, u32[]{:S(2)}) collective-permute-start(bf16[512,128]{1,0:T(8,128)(2,1)S(1)} %get-tuple-element.10), channel_id=1, source_target_pairs={{0,0},{1,1},{2,2},{3,3},{4,4},{5,5},{6,6},{7,7},{8,16},{9,17},{10,... | collective-permute-start | bytes 393224 | tf_op jit(solution)/shard_map/ppermute | solution.py:46
  124.5 1.9 %collective-permute-start.6 = (bf16[512,128]{1,0:T(8,128)(2,1)S(1)}, bf16[512,128]{1,0:T(8,128)(2,1)S(1)}, u32[]{:S(2)}, u32[]{:S(2)}) collective-permute-start(bf16[512,128]{1,0:T(8,128)(2,1)S(1)} %get-tuple-element.11), channel_id=1, source_target_pairs={{0,16},{1,17},{2,18},{3,19},{4,20},{5,21},{6,22},{7,23},{8,0},{9,1... | collective-permute-start | bytes 393224 | tf_op jit(solution)/shard_map/ppermute | solution.py:46
  126.5 0.0 collective-permute-done.7
  126.5 0.0 collective-permute-done.8
  126.5 9.6 %collective-permute-done.5 = bf16[512,128]{1,0:T(8,128)(2,1)S(1)} collective-permute-done((bf16[512,128]{1,0:T(8,128)(2,1)S(1)}, bf16[512,128]{1,0:T(8,128)(2,1)S(1)}, u32[]{:S(2)}, u32[]{:S(2)}) %collective-permute-start.5) | collective-permute-done | bytes 131104 | tf_op jit(solution)/shard_map/ppermute | solution.py:46
  136.1 0.0 collective-permute-done.6
  136.1 0.2 convolution_convert_fusion
  136.4 16.4 %all_to_all.25 = bf16[8,128,128]{2,1,0:T(8,128)(2,1)S(1)} all-to-all(bf16[8,128,128]{2,1,0:T(8,128)(2,1)S(1)} %broadcast_in_dim.53), channel_id=1, replica_groups={{0,16,128,144,256,272,384,400},{32,48,160,176,288,304,416,432},{64,80,1..., dimensions={0} | all-to-all | bytes 524288 | tf_op jit(solution)/shard_map/all_to_all | solution.py:80
  152.9 0.7 broadcast_in_dim.54
  153.5 3.3 %all-to-all-start.4 = ((bf16[4,128,128]{2,1,0:T(8,128)(2,1)}), bf16[4,128,128]{2,1,0:T(8,128)(2,1)S(1)}, u32[]{:S(2)}, u32[]{:S(2)}) async-start(bf16[4,128,128]{2,1,0:T(8,128)(2,1)} %broadcast_in_dim.54), calls=%async_computation.4 | async-start | bytes 262144 | tf_op jit(solution)/shard_map/all_to_all | solution.py:80
  156.9 0.1 broadcast_bitcast_fusion
  156.9 0.8 multiply_convert_fusion
  157.7 3.9 %all-to-all-done.4 = bf16[4,128,128]{2,1,0:T(8,128)(2,1)S(1)} async-done(((bf16[4,128,128]{2,1,0:T(8,128)(2,1)}), bf16[4,128,128]{2,1,0:T(8,128)(2,1)S(1)}, u32[]{:S(2)}, u32[]{:S(2)}) %all-to-all-start.4) | async-done | bytes 131104 | tf_op jit(solution)/shard_map/all_to_all | solution.py:80
  161.7 0.0 copy-done.1
  161.7 0.6 add.75
  (6 shorter events, 0.2 us)
Async XLA Ops:
  4.4 5.8 %copy-start = (bf16[512,128]{1,0:T(8,128)(2,1)S(1)}, bf16[512,128]{1,0:T(8,128)(2,1)}, u32[]{:S(2)}) copy-start(bf16[512,128]{1,0:T(8,128)(2,1)} %param.5) | copy-start | bytes 393220
  4.4 48.2 %all-to-all-start = ((bf16[4,512,1024]{2,1,0:T(8,128)(2,1)}), bf16[4,512,1024]{2,1,0:T(8,128)(2,1)}, u32[]{:S(2)}, u32[]{:S(2)}) async-start(bf16[4,512,1024]{2,1,0:T(8,128)(2,1)} %broadcast_in_dim.23), calls=%async_computation | async-start | bytes 8388608 | tf_op jit(solution)/shard_map/all_to_all | solution.py:80
  10.4 20.1 %collective-permute-start = (bf16[512,128]{1,0:T(8,128)(2,1)S(1)}, bf16[512,128]{1,0:T(8,128)(2,1)S(1)}, u32[]{:S(2)}, u32[]{:S(2)}) collective-permute-start(bf16[512,128]{1,0:T(8,128)(2,1)S(1)} %broadcast_multiply_fusion), channel_id=1, source_target_pairs={{0,0},{1,1},{2,2},{3,3},{4,64},{5,65},{6,66},{7,67},{8,16},{9,17},... | collective-permute-start | bytes 393224 | tf_op jit(solution)/shard_map/ppermute | solution.py:46
  30.4 15.0 %collective-permute-start.3 = (bf16[512,128]{1,0:T(8,128)(2,1)S(1)}, bf16[512,128]{1,0:T(8,128)(2,1)S(1)}, u32[]{:S(2)}, u32[]{:S(2)}) collective-permute-start(bf16[512,128]{1,0:T(8,128)(2,1)S(1)} %collective-permute-done), channel_id=1, source_target_pairs={{0,96},{1,97},{2,98},{3,99},{4,100},{5,101},{6,102},{7,103},{8,104... | collective-permute-start | bytes 393224 | tf_op jit(solution)/shard_map/ppermute | solution.py:46
  40.2 11.9 %collective-permute-start.2 = (bf16[512,128]{1,0:T(8,128)(2,1)S(1)}, bf16[512,128]{1,0:T(8,128)(2,1)S(1)}, u32[]{:S(2)}, u32[]{:S(2)}) collective-permute-start(bf16[512,128]{1,0:T(8,128)(2,1)S(1)} %collective-permute-done), channel_id=1, source_target_pairs={{0,64},{1,65},{2,66},{3,67},{4,68},{5,69},{6,70},{7,71},{8,72},{9,... | collective-permute-start | bytes 393224 | tf_op jit(solution)/shard_map/ppermute | solution.py:46
  42.1 10.0 %collective-permute-start.1 = (bf16[512,128]{1,0:T(8,128)(2,1)S(1)}, bf16[512,128]{1,0:T(8,128)(2,1)S(1)}, u32[]{:S(2)}, u32[]{:S(2)}) collective-permute-start(bf16[512,128]{1,0:T(8,128)(2,1)S(1)} %collective-permute-done), channel_id=1, source_target_pairs={{0,32},{1,33},{2,34},{3,35},{4,36},{5,37},{6,38},{7,39},{8,40},{9,... | collective-permute-start | bytes 393224 | tf_op jit(solution)/shard_map/ppermute | solution.py:46
  52.6 34.6 %collective-permute-start.4 = (bf16[4,512,1024]{2,1,0:T(8,128)(2,1)}, bf16[4,512,1024]{2,1,0:T(8,128)(2,1)}, u32[]{:S(2)}, u32[]{:S(2)}) collective-permute-start(bf16[4,512,1024]{2,1,0:T(8,128)(2,1)} %all-to-all-done.mine), channel_id=1, source_target_pairs={{0,16},{1,17},{2,18},{3,19},{4,20},{5,21},{6,22},{7,23},{8,24},{9,... | collective-permute-start | bytes 12582920 | tf_op jit(solution)/shard_map/ppermute | solution.py:46
  63.1 19.4 %all-to-all-start.2 = ((bf16[4,2,512,128]{3,2,1,0:T(8,128)(2,1)}), bf16[4,2,512,128]{3,2,1,0:T(8,128)(2,1)S(1)}, u32[]{:S(2)}, u32[]{:S(2)}) async-start(bf16[4,2,512,128]{3,2,1,0:T(8,128)(2,1)} %broadcast_in_dim.50), calls=%async_computation.2 | async-start | bytes 2097152 | tf_op jit(solution)/shard_map/all_to_all | solution.py:80
  83.6 27.2 %all-to-all-start.1 = ((bf16[4,2,512,128]{3,2,1,0:T(8,128)(2,1)}), bf16[4,2,512,128]{3,2,1,0:T(8,128)(2,1)S(1)}, u32[]{:S(2)}, u32[]{:S(2)}) async-start(bf16[4,2,512,128]{3,2,1,0:T(8,128)(2,1)} %broadcast_in_dim.24), calls=%async_computation.1 | async-start | bytes 2097152 | tf_op jit(solution)/shard_map/all_to_all | solution.py:80
  93.2 33.3 %collective-permute-start.7 = (bf16[512,128]{1,0:T(8,128)(2,1)S(1)}, bf16[512,128]{1,0:T(8,128)(2,1)S(1)}, u32[]{:S(2)}, u32[]{:S(2)}) collective-permute-start(bf16[512,128]{1,0:T(8,128)(2,1)S(1)} %get-tuple-element.12), channel_id=1, source_target_pairs={{0,4},{1,5},{2,6},{3,7},{4,0},{5,1},{6,2},{7,3},{8,20},{9,21},{10,... | collective-permute-start | bytes 393224 | tf_op jit(solution)/shard_map/ppermute | solution.py:46
  106.7 19.8 %collective-permute-start.8 = (bf16[512,128]{1,0:T(8,128)(2,1)S(1)}, bf16[512,128]{1,0:T(8,128)(2,1)S(1)}, u32[]{:S(2)}, u32[]{:S(2)}) collective-permute-start(bf16[512,128]{1,0:T(8,128)(2,1)S(1)} %get-tuple-element.13), channel_id=1, source_target_pairs={{0,20},{1,21},{2,22},{3,23},{4,16},{5,17},{6,18},{7,19},{8,4},{9,5... | collective-permute-start | bytes 393224 | tf_op jit(solution)/shard_map/ppermute | solution.py:46
  110.9 50.8 %copy-start.1 = (f32[128,128]{1,0:T(8,128)S(1)}, f32[128,128]{1,0:T(8,128)}, u32[]{:S(2)}) copy-start(f32[128,128]{1,0:T(8,128)} %param.7) | copy-start | bytes 196612
  116.9 19.2 %collective-permute-start.5 = (bf16[512,128]{1,0:T(8,128)(2,1)S(1)}, bf16[512,128]{1,0:T(8,128)(2,1)S(1)}, u32[]{:S(2)}, u32[]{:S(2)}) collective-permute-start(bf16[512,128]{1,0:T(8,128)(2,1)S(1)} %get-tuple-element.10), channel_id=1, source_target_pairs={{0,0},{1,1},{2,2},{3,3},{4,4},{5,5},{6,6},{7,7},{8,16},{9,17},{10,... | collective-permute-start | bytes 393224 | tf_op jit(solution)/shard_map/ppermute | solution.py:46
  124.5 11.6 %collective-permute-start.6 = (bf16[512,128]{1,0:T(8,128)(2,1)S(1)}, bf16[512,128]{1,0:T(8,128)(2,1)S(1)}, u32[]{:S(2)}, u32[]{:S(2)}) collective-permute-start(bf16[512,128]{1,0:T(8,128)(2,1)S(1)} %get-tuple-element.11), channel_id=1, source_target_pairs={{0,16},{1,17},{2,18},{3,19},{4,20},{5,21},{6,22},{7,23},{8,0},{9,1... | collective-permute-start | bytes 393224 | tf_op jit(solution)/shard_map/ppermute | solution.py:46
  153.5 8.1 %all-to-all-start.4 = ((bf16[4,128,128]{2,1,0:T(8,128)(2,1)}), bf16[4,128,128]{2,1,0:T(8,128)(2,1)S(1)}, u32[]{:S(2)}, u32[]{:S(2)}) async-start(bf16[4,128,128]{2,1,0:T(8,128)(2,1)} %broadcast_in_dim.54), calls=%async_computation.4 | async-start | bytes 262144 | tf_op jit(solution)/shard_map/all_to_all | solution.py:80

commit v3 on v1

v3 whole, which is shorter than its diff:
```python
import jax
import jax.numpy as jnp
from jax import lax
from jax.experimental import pallas as pl
from jax.experimental.pallas import tpu as pltpu
from jax.sharding import PartitionSpec as P

W = 128
BF = jnp.bfloat16
F32 = jnp.float32
PROW, PCOL = 32, 16
BOTH = ("prow", "pcol")


def groups(count, key):
    found = {}
    for i in range(count):
        found.setdefault(key(i), []).append(i)
    return list(found.values())


ZLO = groups(PROW, lambda r: (r // 8, r % 2))
Y = groups(PROW, lambda r: r % 8)
YC = groups(PROW, lambda r: r // 2 % 4)


def place(y, z_lo, core, z_hi, x):
    return ((y * 4 + z_lo) * 2 + core) * PCOL + z_hi * 4 + x


def moves(to):
    pairs = []
    for device in range(PROW * PCOL):
        r, c = divmod(device, PCOL)
        where = to(r // 8, r // 2 % 4, r % 2, c // 4, c % 4)
        if where is not None:
            pairs.append((device, place(*where)))
    return pairs


def send(block, to):
    return lax.ppermute(block, BOTH, moves(to))


def spread_y(y, z_lo, core, z_hi, x):
    return (y + z_lo) % 4, z_lo, core, z_hi, x


def spread_z(y, z_lo, core, z_hi, x):
    return y, 2 * (z_hi % 2) + core, z_hi // 2, (y - z_lo) % 4, x


def swap(y, z_lo, core, z_hi, x):
    return y, z_lo, 1 - core, z_hi, x


def along_x(d):
    return lambda y, z_lo, core, z_hi, x: (y, z_lo, core, z_hi, (x + d) % 4)


def relay(step):
    def to(y, z_lo, core, z_hi, x):
        if core != z_hi // 2:
            return y, z_lo, core, (z_hi + step) % 4, x
        if z_hi % 2 == (step < 0):
            return y, z_lo, 1 - core, z_hi, x
        return None

    return to


def onward(relayed):
    def to(y, z_lo, core, z_hi, x):
        target = 2 * core + 1 - z_hi % 2
        rising = target == (z_hi + 1) % 4
        return y, z_lo, int(rising != relayed), target, x

    return to


def gather(block, axis, members):
    count = len(members[0])
    copies = jnp.broadcast_to(block[None], (count,) + block.shape)
    return lax.all_to_all(copies, axis, 0, 0, axis_index_groups=members)


def times_kernel(order, panel, *refs):
    ours, others, (out, panel_here, parts, total, sems) = refs[:5], refs[5:10], refs[10:]
    rows, half = parts.shape[1], parts.shape[1] // 2
    copies = [[pltpu.make_async_copy(panel, panel_here, sems.at[0])]]
    for d in range(4):
        pairs = []
        for core, blocks in enumerate((ours, others)):
            slot = parts.at[2 * d + core]
            if d < 3:
                pairs.append((blocks[d], slot))
            else:
                pairs += [(blocks[3], slot.at[pl.ds(0, half)]), (blocks[4], slot.at[pl.ds(half, half)])]
        first = sum(len(group) for group in copies)
        copies.append([pltpu.make_async_copy(a, b, sems.at[first + i]) for i, (a, b) in enumerate(pairs)])
    for group in copies:
        for copy in group:
            copy.start()
    for copy in copies[0]:
        copy.wait()
    for d in range(4):
        for copy in copies[d + 1]:
            copy.wait()
        columns = jnp.concatenate([panel_here[order[d], 0], panel_here[order[d], 1]], axis=1)
        for core in range(2):
            here = pl.ds(core * rows, rows)
            term = jnp.dot(parts[2 * d + core], columns, preferred_element_type=F32)
            total[here] = term if d == 0 else total[here] + term
    for core in range(2):
        for b in range(2):
            slot = jnp.where(order[4] == b, order[5], order[6])
            out[slot ^ core] = total[pl.ds(core * rows, rows), pl.ds(b * W, W)].astype(BF)


def times(order, ours, others, panel):
    rows, depth = ours[0].shape
    return pl.pallas_call(
        times_kernel,
        in_specs=[pl.BlockSpec(memory_space=pltpu.SMEM)] + [pl.BlockSpec(memory_space=pl.ANY)] * 11,
        out_specs=pl.BlockSpec(memory_space=pltpu.VMEM),
        out_shape=jax.ShapeDtypeStruct((4, rows, W), BF),
        scratch_shapes=[
            pltpu.VMEM(panel.shape, BF),
            pltpu.VMEM((8, rows, depth), BF),
            pltpu.VMEM((2 * rows, 2 * W), F32),
            pltpu.SemaphoreType.DMA((11,)),
        ],
        compiler_params=pltpu.CompilerParams(vmem_limit_bytes=56 * 1024 * 1024),
        cost_estimate=pl.CostEstimate(
            flops=32 * rows * depth * W, bytes_accessed=18 * rows * depth, transcendentals=0
        ),
    )(order, panel, *ours, *others)


def on_device(ancestor_inverse, factor_panel, pattern, diagonal_term):
    row_index = lax.axis_index("prow")
    col_index = lax.axis_index("pcol")
    y, z_lo, core = row_index // 8, row_index // 2 % 4, row_index % 2
    z_hi, x = col_index // 4, col_index % 4
    rows = factor_panel.shape[0]
    row_blocks = rows // W
    local_mask = lax.dynamic_slice(
        pattern, (row_index * row_blocks, col_index), (row_blocks, 1)
    )
    expanded = jnp.broadcast_to(local_mask[:, :, None], (row_blocks, W, W)).reshape(rows, W)
    masked = factor_panel * expanded.astype(BF)
    ancestor_inverse, masked = lax.optimization_barrier((ancestor_inverse, masked))
    half = rows // 2
    before = send(ancestor_inverse, along_x(1))
    after = send(ancestor_inverse, along_x(3))
    block = send(send(masked, spread_y), spread_z)
    block, before, after = lax.optimization_barrier((block, before, after))
    near = gather(block, "prow", ZLO)
    swapped = [send(part, swap) for part in (ancestor_inverse, before, after)]
    near, *swapped = lax.optimization_barrier((near, *swapped))
    panel = gather(near, "prow", Y).reshape(4, 2, 2 * rows, W)
    top = send(before[:half], along_x(1))
    bottom = send(after[half:], along_x(3))
    ours = [ancestor_inverse, before, after, top, bottom]
    others = swapped + [send(part, swap) for part in ours[3:]]
    stays = core == z_hi // 2
    rising = 2 * core + 1 - z_hi % 2 == (z_hi + 1) % 4
    order = jnp.stack(
        [(x - d + z_hi) % 4 for d in (0, 1, 3, 2)]
        + [z_hi % 2, jnp.where(stays, 1 - z_hi % 2, core), jnp.where(rising == (core == 0), 3, 2)]
    )
    up, down, direct, last = times(order, ours, others, panel)
    from_below, from_above = send(up, relay(1)), send(down, relay(-1))
    product = send(direct, onward(False)).astype(F32)
    kept = jnp.where(stays, jnp.where(z_hi % 2 == 0, down, up), jnp.where(rising, from_above, from_below))
    relayed = jnp.where(rising, from_below, from_above)
    last = (last.astype(F32) + relayed.astype(F32)).astype(BF)
    product += kept.astype(F32) + send(last, onward(True)).astype(F32)
    offdiag = (-product * expanded.astype(F32)).astype(BF)
    sums = lax.dot_general(
        masked, product.astype(BF), (((0,), (0,)), ((), ())), preferred_element_type=F32
    )
    for members in (YC, ZLO):
        sums = jnp.sum(gather(sums.astype(BF), "prow", members).astype(F32), axis=0)
    return offdiag, diagonal_term + sums


def solution(mesh):
    in_specs = (P("prow", "pcol"), P("prow", "pcol"), P(), P("pcol", None))
    out_specs = (P("prow", "pcol"), P("pcol", None))
    return jax.shard_map(
        on_device, mesh=mesh, in_specs=in_specs, out_specs=out_specs, check_vma=False
    )
```

time: 187 us -> 156 us (0.83)
  blocking collectives: 85.6 us -> 28 us
  starting transfers between devices: 36.1 us -> 79.4 us
  waiting for transfers between devices: 52 us -> 25.6 us
  Pallas kernels: 0 us -> 6.3 us
  local copies, waits for them, and re-layouts: 3.36 us -> 8.86 us
  matrix products: 4.66 us -> 0.23 us
    all_to_all x2 -> x0, blocking collectives: 63.1 us -> none  [the longest x1 34.5 us: on_device(): partial = lax.all_to_all(partial, 'pcol', 0, 0, axis_index_groups=ZHI)]
    ppermute x3 -> x15, starting transfers between devices: 14.3 us -> 63.9 us  [send(): return lax.ppermute(block, BOTH, moves(to))]
    all_to_all x1 -> x2, waiting for transfers between devices: 21.4 us -> 4.67 us  [gather(): return lax.all_to_all(copies, axis, 0, 0, axis_index_groups=members)]
    all_to_all x2 -> x0, waiting for transfers between devices: 14.3 us -> none  [the longest x1 7.45 us: on_device(): pieces = lax.all_to_all(pieces, 'prow', 0, 0)]
    all_to_all x2 -> x0, starting transfers between devices: 12.7 us -> none  [the longest x1 8.61 us: on_device(): pieces = lax.all_to_all(pieces, 'prow', 0, 0)]
    pallas_call x0 -> x1, Pallas kernels: none -> 6.3 us  [times(): pl.pallas_call(times_kernel, in_specs=[pl.BlockSpec(memory_space=pltpu.SM...]
    all_to_all x1 -> x2, starting transfers between devices: 9.21 us -> 15.4 us  [gather(): return lax.all_to_all(copies, axis, 0, 0, axis_index_groups=members)]
    all_to_all x1 -> x2, blocking collectives: 22.5 us -> 28 us  [gather(): return lax.all_to_all(copies, axis, 0, 0, axis_index_groups=members)]
  transfers between devices with their start and end apart: 6 -> 17, of which waited for: 5 -> 9; matrix products, arithmetic and copies ran while one was open for 1% -> 2% of each run, Pallas kernels for 0% -> 0%
where the time goes in v3:
time: 156 us; the launch traced here: 155 us
  starting transfers between devices  79.4 us (51%)
  blocking collectives  28 us (18%)
  waiting for transfers between devices  25.6 us (16%)
  local copies, waits for them, and re-layouts  8.86 us (6%)
  Pallas kernels  6.3 us (4%)
  other arithmetic  5.22 us (3%)
    ppermute x15, starting transfers between devices, send(): return lax.ppermute(block, BOTH, moves(to))  63.9 us
    all_to_all x2, blocking collectives, gather(): return lax.all_to_all(copies, axis, 0, 0, axis_index_groups=members)  28 us
    ppermute x15, waiting for transfers between devices, send(): return lax.ppermute(block, BOTH, moves(to))  20.9 us
    all_to_all x2, starting transfers between devices, gather(): return lax.all_to_all(copies, axis, 0, 0, axis_index_groups=members)  15.4 us
    pallas_call x1, Pallas kernels, times(): pl.pallas_call(times_kernel, in_specs=[pl.BlockSpec(memory_space=pltpu.SM...  6.3 us
    all_to_all x2, waiting for transfers between devices, gather(): return lax.all_to_all(copies, axis, 0, 0, axis_index_groups=members)  4.67 us
    unnamed x16, local copies, waits for them, and re-layouts  3.15 us
  transfers between devices with their start and end apart: 17, of which 9 were waited for; matrix products, arithmetic and copies ran while one was open for 2% of the time, Pallas kernels for 0%

profile of v3, /device:TPU:1, one launch (start us, length us, event | category | flops | bytes accessed | tf_op | source)
XLA Modules:
  0.0 154.7 jit_solution(10188019770446312421)
XLA Ops:
  0.6 0.8 convert_bitcast_fusion
  1.4 0.1 broadcast_bitcast_fusion.1
  1.5 1.0 broadcast_multiply_fusion
  2.5 4.0 %collective-permute-start.2 = (bf16[512,1024]{1,0:T(8,128)(2,1)}, bf16[512,1024]{1,0:T(8,128)(2,1)S(1)}, u32[]{:S(2)}, u32[]{:S(2)}) collective-permute-start(bf16[512,1024]{1,0:T(8,128)(2,1)} %refs_0_), channel_id=1, source_target_pairs={{0,1},{1,2},{2,3},{3,0},{4,5},{5,6},{6,7},{7,4},{8,9},{9,10},{10,1... | collective-permute-start | bytes 3145736 | tf_op jit(solution)/shard_map/ppermute | solution.py:42
  6.5 3.2 %collective-permute-start.3 = (bf16[512,1024]{1,0:T(8,128)(2,1)}, bf16[512,1024]{1,0:T(8,128)(2,1)S(1)}, u32[]{:S(2)}, u32[]{:S(2)}) collective-permute-start(bf16[512,1024]{1,0:T(8,128)(2,1)} %refs_0_), channel_id=1, source_target_pairs={{0,3},{1,0},{2,1},{3,2},{4,7},{5,4},{6,5},{7,6},{8,11},{9,8},{10,9... | collective-permute-start | bytes 3145736 | tf_op jit(solution)/shard_map/ppermute | solution.py:42
  9.7 0.7 collective-permute-start
  10.4 12.2 %collective-permute-start.1 = (bf16[512,128]{1,0:T(8,128)(2,1)S(1)}, bf16[512,128]{1,0:T(8,128)(2,1)S(1)}, u32[]{:S(2)}, u32[]{:S(2)}) collective-permute-start(bf16[512,128]{1,0:T(8,128)(2,1)S(1)} %collective-permute-done), channel_id=1, source_target_pairs={{0,0},{1,1},{2,2},{3,3},{4,64},{5,65},{6,66},{7,67},{8,16},{9,17},... | collective-permute-start | bytes 393224 | tf_op jit(solution)/shard_map/ppermute | solution.py:42
  22.6 7.3 %collective-permute-done.1 = bf16[512,128]{1,0:T(8,128)(2,1)S(1)} collective-permute-done((bf16[512,128]{1,0:T(8,128)(2,1)S(1)}, bf16[512,128]{1,0:T(8,128)(2,1)S(1)}, u32[]{:S(2)}, u32[]{:S(2)}) %collective-permute-start.1) | collective-permute-done | bytes 131104 | tf_op jit(solution)/shard_map/ppermute | solution.py:42
  29.9 1.0 broadcast_in_dim.18
  30.8 8.6 %all-to-all-start = ((bf16[4,512,128]{2,1,0:T(8,128)(2,1)}), bf16[4,512,128]{2,1,0:T(8,128)(2,1)S(1)}, u32[]{:S(2)}, u32[]{:S(2)}) async-start(bf16[4,512,128]{2,1,0:T(8,128)(2,1)} %broadcast_in_dim.18), calls=%async_computation | async-start | bytes 1048576 | tf_op jit(solution)/shard_map/all_to_all | solution.py:84
  39.4 3.5 %collective-permute-start.4 = (bf16[512,1024]{1,0:T(8,128)(2,1)}, bf16[512,1024]{1,0:T(8,128)(2,1)S(1)}, u32[]{:S(2)}, u32[]{:S(2)}) collective-permute-start(bf16[512,1024]{1,0:T(8,128)(2,1)} %refs_0_), channel_id=1, source_target_pairs={{0,16},{1,17},{2,18},{3,19},{4,20},{5,21},{6,22},{7,23},{8,24},{9,... | collective-permute-start | bytes 3145736 | tf_op jit(solution)/shard_map/ppermute | solution.py:42
  42.9 1.9 %collective-permute-start.5 = (bf16[512,1024]{1,0:T(8,128)(2,1)S(1)}, bf16[512,1024]{1,0:T(8,128)(2,1)S(1)}, u32[]{:S(2)}, u32[]{:S(2)}) collective-permute-start(bf16[512,1024]{1,0:T(8,128)(2,1)S(1)} %collective-permute-done.2.refs_1_), channel_id=1, source_target_pairs={{0,16},{1,17},{2,18},{3,19},{4,20},{5,21},{6,22},{7,23},{8,24},{9,... | collective-permute-start | bytes 3145736 | tf_op jit(solution)/shard_map/ppermute | solution.py:42
  44.8 2.4 %collective-permute-start.6 = (bf16[512,1024]{1,0:T(8,128)(2,1)S(1)}, bf16[512,1024]{1,0:T(8,128)(2,1)}, u32[]{:S(2)}, u32[]{:S(2)}) collective-permute-start(bf16[512,1024]{1,0:T(8,128)(2,1)S(1)} %collective-permute-done.3.refs_2_), channel_id=1, source_target_pairs={{0,16},{1,17},{2,18},{3,19},{4,20},{5,21},{6,22},{7,23},{8,24},{9,... | collective-permute-start | bytes 3145736 | tf_op jit(solution)/shard_map/ppermute | solution.py:42
  47.3 0.2 collective-permute-done.5.refs_6_
  47.5 0.8 copy-done.3
  48.3 1.0 copy-done.4
  49.3 0.4 collective-permute-done.6.refs_7_
  49.7 3.7 %all-to-all-done = bf16[4,512,128]{2,1,0:T(8,128)(2,1)S(1)} async-done(((bf16[4,512,128]{2,1,0:T(8,128)(2,1)}), bf16[4,512,128]{2,1,0:T(8,128)(2,1)S(1)}, u32[]{:S(2)}, u32[]{:S(2)}) %all-to-all-start) | async-done | bytes 524320 | tf_op jit(solution)/shard_map/all_to_all | solution.py:84
  53.4 1.8 %broadcast_in_dim.19 = bf16[4,4,512,128]{3,2,1,0:T(8,128)(2,1)} broadcast(bf16[4,512,128]{2,1,0:T(8,128)(2,1)S(1)} %all-to-all-done), dimensions={1,2,3} | broadcast | bytes 2621440 | tf_op jit(solution)/shard_map/broadcast_in_dim | solution.py:83
  55.2 6.9 %all-to-all-start.1 = ((bf16[4,4,512,128]{3,2,1,0:T(8,128)(2,1)}), bf16[4,4,512,128]{3,2,1,0:T(8,128)(2,1)S(1)}, u32[]{:S(2)}, u32[]{:S(2)}) async-start(bf16[4,4,512,128]{3,2,1,0:T(8,128)(2,1)} %broadcast_in_dim.19), calls=%async_computation.1 | async-start | bytes 4194304 | tf_op jit(solution)/shard_map/all_to_all | solution.py:84
  62.0 1.1 slice.7
  63.1 2.7 %collective-permute-start.8 = (bf16[256,1024]{1,0:T(8,128)(2,1)S(1)}, bf16[256,1024]{1,0:T(8,128)(2,1)}, u32[]{:S(2)}, u32[]{:S(2)}) collective-permute-start(bf16[256,1024]{1,0:T(8,128)(2,1)S(1)} %slice.7), channel_id=1, source_target_pairs={{0,3},{1,0},{2,1},{3,2},{4,7},{5,4},{6,5},{7,6},{8,11},{9,8},{10,9... | collective-permute-start | bytes 1572872 | tf_op jit(solution)/shard_map/ppermute | solution.py:42
  65.8 2.6 %collective-permute-start.7 = (bf16[256,1024]{1,0:T(8,128)(2,1)S(1)}, bf16[256,1024]{1,0:T(8,128)(2,1)S(1)}, u32[]{:S(2)}, u32[]{:S(2)}) collective-permute-start(bf16[256,1024]{1,0:T(8,128)(2,1)S(1)} %slice.6), channel_id=1, source_target_pairs={{0,1},{1,2},{2,3},{3,0},{4,5},{5,6},{6,7},{7,4},{8,9},{9,10},{10,1... | collective-permute-start | bytes 1572872 | tf_op jit(solution)/shard_map/ppermute | solution.py:42
  68.5 9.4 %collective-permute-done.8.refs_4_ = bf16[256,1024]{1,0:T(8,128)(2,1)} collective-permute-done((bf16[256,1024]{1,0:T(8,128)(2,1)S(1)}, bf16[256,1024]{1,0:T(8,128)(2,1)}, u32[]{:S(2)}, u32[]{:S(2)}) %collective-permute-start.8) | collective-permute-done | bytes 524320 | tf_op jit(solution)/shard_map/ppermute | solution.py:42
  77.9 3.4 %collective-permute-start.10 = (bf16[256,1024]{1,0:T(8,128)(2,1)}, bf16[256,1024]{1,0:T(8,128)(2,1)S(1)}, u32[]{:S(2)}, u32[]{:S(2)}) collective-permute-start(bf16[256,1024]{1,0:T(8,128)(2,1)} %collective-permute-done.8.refs_4_), channel_id=1, source_target_pairs={{0,16},{1,17},{2,18},{3,19},{4,20},{5,21},{6,22},{7,23},{8,24},{9,... | collective-permute-start | bytes 1572872 | tf_op jit(solution)/shard_map/ppermute | solution.py:42
  81.4 3.8 %collective-permute-start.9 = (bf16[256,1024]{1,0:T(8,128)(2,1)S(1)}, bf16[256,1024]{1,0:T(8,128)(2,1)}, u32[]{:S(2)}, u32[]{:S(2)}) collective-permute-start(bf16[256,1024]{1,0:T(8,128)(2,1)S(1)} %collective-permute-done.7.refs_3_), channel_id=1, source_target_pairs={{0,16},{1,17},{2,18},{3,19},{4,20},{5,21},{6,22},{7,23},{8,24},{9,... | collective-permute-start | bytes 1572872 | tf_op jit(solution)/shard_map/ppermute | solution.py:42
  85.3 0.6 stack.31.order
  86.0 0.0 collective-permute-done.10.refs_9_
  86.0 0.9 collective-permute-done.9.refs_8_
  86.8 0.9 all-to-all-done.1
  87.8 1.3 copy-done
  89.1 6.3 %shard_map.59 = bf16[4,512,128]{2,1,0:T(8,128)(2,1)} custom-call(s32[7]{0:T(128)} %stack.31.order, bf16[4,2,1024,128]{3,2,1,0:T(8,128)(2,1)} %bitcast.34, bf16[512,1024]{1,0:T(8,128)(2,1)} %refs_0_, bf16[512,1024]{1,0:T(8,128)(2,1)} %copy-done.1, bf16[512,1024]{1,0:T(8,128)(2,1)} %copy-done.2, bf16[256,1024]{1,0:T(8,128)(2,1)} %copy-done.5, ...), custom_call_target="tpu_custom_call" | custom-call | flops 2147483648 | bytes 9437184 | tf_op jit(solution)/shard_map/pallas_call | solution.py:122
  95.4 1.1 slice_bitcast_fusion.3
  96.5 0.0 copy-start.7
  96.5 8.0 %collective-permute-start.12 = (bf16[512,128]{1,0:T(8,128)(2,1)S(1)}, bf16[512,128]{1,0:T(8,128)(2,1)S(1)}, u32[]{:S(2)}, u32[]{:S(2)}) collective-permute-start(bf16[512,128]{1,0:T(8,128)(2,1)S(1)} %get-tuple-element.24), channel_id=1, source_target_pairs={{4,20},{5,21},{6,22},{7,23},{8,4},{9,5},{10,6},{11,7},{12,8},{13,9... | collective-permute-start | bytes 393224 | tf_op jit(solution)/shard_map/ppermute | solution.py:42
  104.5 1.9 %collective-permute-start.13 = (bf16[512,128]{1,0:T(8,128)(2,1)S(1)}, bf16[512,128]{1,0:T(8,128)(2,1)S(1)}, u32[]{:S(2)}, u32[]{:S(2)}) collective-permute-start(bf16[512,128]{1,0:T(8,128)(2,1)S(1)} %get-tuple-element.23), channel_id=1, source_target_pairs={{0,16},{1,17},{2,18},{3,19},{8,12},{9,13},{10,14},{11,15},{12,0},{... | collective-permute-start | bytes 393224 | tf_op jit(solution)/shard_map/ppermute | solution.py:42
  106.4 6.1 %collective-permute-start.11 = (bf16[512,128]{1,0:T(8,128)(2,1)S(1)}, bf16[512,128]{1,0:T(8,128)(2,1)S(1)}, u32[]{:S(2)}, u32[]{:S(2)}) collective-permute-start(bf16[512,128]{1,0:T(8,128)(2,1)S(1)} %get-tuple-element.22), channel_id=1, source_target_pairs={{0,20},{1,21},{2,22},{3,23},{4,0},{5,1},{6,2},{7,3},{8,4},{9,5},{1... | collective-permute-start | bytes 393224 | tf_op jit(solution)/shard_map/ppermute | solution.py:42
  112.5 0.0 collective-permute-done.12
  112.5 1.0 fusion
  113.5 7.5 %collective-permute-start.14 = (bf16[512,128]{1,0:T(8,128)(2,1)S(1)}, bf16[512,128]{1,0:T(8,128)(2,1)S(1)}, u32[]{:S(2)}, u32[]{:S(2)}) collective-permute-start(bf16[512,128]{1,0:T(8,128)(2,1)S(1)} %fusion), channel_id=1, source_target_pairs={{0,4},{1,5},{2,6},{3,7},{4,16},{5,17},{6,18},{7,19},{8,20},{9,21},... | collective-permute-start | bytes 393224 | tf_op jit(solution)/shard_map/ppermute | solution.py:42
  121.1 0.1 broadcast_bitcast_fusion
  121.1 0.9 collective-permute-done.11
  122.1 1.8 %collective-permute-done.14 = bf16[512,128]{1,0:T(8,128)(2,1)S(1)} collective-permute-done((bf16[512,128]{1,0:T(8,128)(2,1)S(1)}, bf16[512,128]{1,0:T(8,128)(2,1)S(1)}, u32[]{:S(2)}, u32[]{:S(2)}) %collective-permute-start.14) | collective-permute-done | bytes 131104 | tf_op jit(solution)/shard_map/ppermute | solution.py:42
  123.9 1.8 %multiply_convert_fusion = (bf16[512,128]{1,0:T(8,128)(2,1)}, bf16[512,128]{1,0:T(8,128)(2,1)S(1)}) fusion(bf16[512,128]{1,0:T(8,128)(2,1)S(1)} %collective-permute-done.14, bf16[512,128]{1,0:T(8,128)(2,1)S(1)} %collective-permute-done.11, f32[512]{0:T(512)S(1)} %broadcast_bitcast_fusion, bf16[512,128]{1,0:T(8,128)(2,1)S(1)} %collective-permute-done.12, ...), kind=kLoop, calls=%fused_computation.4 | loop fusion | flops 720896 | bytes 1050627 | tf_op jit(solution)/shard_map/convert_element_type | solution.py:179
  125.7 0.2 convolution_convert_fusion
  125.9 20.7 %all_to_all.20 = bf16[8,128,128]{2,1,0:T(8,128)(2,1)S(1)} all-to-all(bf16[8,128,128]{2,1,0:T(8,128)(2,1)S(1)} %broadcast_in_dim.42), channel_id=1, replica_groups={{0,16,128,144,256,272,384,400},{32,48,160,176,288,304,416,432},{64,80,1..., dimensions={0} | all-to-all | bytes 524288 | tf_op jit(solution)/shard_map/all_to_all | solution.py:84
  146.7 7.3 %all_to_all.21 = bf16[4,128,128]{2,1,0:T(8,128)(2,1)S(1)} all-to-all(bf16[4,128,128]{2,1,0:T(8,128)(2,1)S(1)} %broadcast_in_dim.43), channel_id=1, replica_groups={{0,32,64,96},{16,48,80,112},{128,160,192,224},{144,176,208,240},{256,28..., dimensions={0} | all-to-all | bytes 262144 | tf_op jit(solution)/shard_map/all_to_all | solution.py:84
  154.1 0.6 add.88
  (23 shorter events, 0.2 us)
Async XLA Ops:
  2.5 27.3 %collective-permute-start.2 = (bf16[512,1024]{1,0:T(8,128)(2,1)}, bf16[512,1024]{1,0:T(8,128)(2,1)S(1)}, u32[]{:S(2)}, u32[]{:S(2)}) collective-permute-start(bf16[512,1024]{1,0:T(8,128)(2,1)} %refs_0_), channel_id=1, source_target_pairs={{0,1},{1,2},{2,3},{3,0},{4,5},{5,6},{6,7},{7,4},{8,9},{9,10},{10,1... | collective-permute-start | bytes 3145736 | tf_op jit(solution)/shard_map/ppermute | solution.py:42
  6.5 23.4 %collective-permute-start.3 = (bf16[512,1024]{1,0:T(8,128)(2,1)}, bf16[512,1024]{1,0:T(8,128)(2,1)S(1)}, u32[]{:S(2)}, u32[]{:S(2)}) collective-permute-start(bf16[512,1024]{1,0:T(8,128)(2,1)} %refs_0_), channel_id=1, source_target_pairs={{0,3},{1,0},{2,1},{3,2},{4,7},{5,4},{6,5},{7,6},{8,11},{9,8},{10,9... | collective-permute-start | bytes 3145736 | tf_op jit(solution)/shard_map/ppermute | solution.py:42
  9.7 0.7 collective-permute-start
  10.4 19.5 %collective-permute-start.1 = (bf16[512,128]{1,0:T(8,128)(2,1)S(1)}, bf16[512,128]{1,0:T(8,128)(2,1)S(1)}, u32[]{:S(2)}, u32[]{:S(2)}) collective-permute-start(bf16[512,128]{1,0:T(8,128)(2,1)S(1)} %collective-permute-done), channel_id=1, source_target_pairs={{0,0},{1,1},{2,2},{3,3},{4,64},{5,65},{6,66},{7,67},{8,16},{9,17},... | collective-permute-start | bytes 393224 | tf_op jit(solution)/shard_map/ppermute | solution.py:42
  29.9 35.9 %copy-start.1 = (bf16[512,1024]{1,0:T(8,128)(2,1)}, bf16[512,1024]{1,0:T(8,128)(2,1)S(1)}, u32[]{:S(2)}) copy-start(bf16[512,1024]{1,0:T(8,128)(2,1)S(1)} %collective-permute-done.2.refs_1_) | copy-start | bytes 3145732
  29.9 25.3 %copy-start.2 = (bf16[512,1024]{1,0:T(8,128)(2,1)}, bf16[512,1024]{1,0:T(8,128)(2,1)S(1)}, u32[]{:S(2)}) copy-start(bf16[512,1024]{1,0:T(8,128)(2,1)S(1)} %collective-permute-done.3.refs_2_) | copy-start | bytes 3145732
  30.8 22.6 %all-to-all-start = ((bf16[4,512,128]{2,1,0:T(8,128)(2,1)}), bf16[4,512,128]{2,1,0:T(8,128)(2,1)S(1)}, u32[]{:S(2)}, u32[]{:S(2)}) async-start(bf16[4,512,128]{2,1,0:T(8,128)(2,1)} %broadcast_in_dim.18), calls=%async_computation | async-start | bytes 1048576 | tf_op jit(solution)/shard_map/all_to_all | solution.py:84
  39.4 7.9 %collective-permute-start.4 = (bf16[512,1024]{1,0:T(8,128)(2,1)}, bf16[512,1024]{1,0:T(8,128)(2,1)S(1)}, u32[]{:S(2)}, u32[]{:S(2)}) collective-permute-start(bf16[512,1024]{1,0:T(8,128)(2,1)} %refs_0_), channel_id=1, source_target_pairs={{0,16},{1,17},{2,18},{3,19},{4,20},{5,21},{6,22},{7,23},{8,24},{9,... | collective-permute-start | bytes 3145736 | tf_op jit(solution)/shard_map/ppermute | solution.py:42
  42.9 4.6 %collective-permute-start.5 = (bf16[512,1024]{1,0:T(8,128)(2,1)S(1)}, bf16[512,1024]{1,0:T(8,128)(2,1)S(1)}, u32[]{:S(2)}, u32[]{:S(2)}) collective-permute-start(bf16[512,1024]{1,0:T(8,128)(2,1)S(1)} %collective-permute-done.2.refs_1_), channel_id=1, source_target_pairs={{0,16},{1,17},{2,18},{3,19},{4,20},{5,21},{6,22},{7,23},{8,24},{9,... | collective-permute-start | bytes 3145736 | tf_op jit(solution)/shard_map/ppermute | solution.py:42
  44.8 4.8 %collective-permute-start.6 = (bf16[512,1024]{1,0:T(8,128)(2,1)S(1)}, bf16[512,1024]{1,0:T(8,128)(2,1)}, u32[]{:S(2)}, u32[]{:S(2)}) collective-permute-start(bf16[512,1024]{1,0:T(8,128)(2,1)S(1)} %collective-permute-done.3.refs_2_), channel_id=1, source_target_pairs={{0,16},{1,17},{2,18},{3,19},{4,20},{5,21},{6,22},{7,23},{8,24},{9,... | collective-permute-start | bytes 3145736 | tf_op jit(solution)/shard_map/ppermute | solution.py:42
  47.3 1.0 copy-start.3
  48.3 1.0 copy-start.4
  55.2 32.6 %all-to-all-start.1 = ((bf16[4,4,512,128]{3,2,1,0:T(8,128)(2,1)}), bf16[4,4,512,128]{3,2,1,0:T(8,128)(2,1)S(1)}, u32[]{:S(2)}, u32[]{:S(2)}) async-start(bf16[4,4,512,128]{3,2,1,0:T(8,128)(2,1)} %broadcast_in_dim.19), calls=%async_computation.1 | async-start | bytes 4194304 | tf_op jit(solution)/shard_map/all_to_all | solution.py:84
  63.1 14.8 %collective-permute-start.8 = (bf16[256,1024]{1,0:T(8,128)(2,1)S(1)}, bf16[256,1024]{1,0:T(8,128)(2,1)}, u32[]{:S(2)}, u32[]{:S(2)}) collective-permute-start(bf16[256,1024]{1,0:T(8,128)(2,1)S(1)} %slice.7), channel_id=1, source_target_pairs={{0,3},{1,0},{2,1},{3,2},{4,7},{5,4},{6,5},{7,6},{8,11},{9,8},{10,9... | collective-permute-start | bytes 1572872 | tf_op jit(solution)/shard_map/ppermute | solution.py:42
  65.8 15.5 %collective-permute-start.7 = (bf16[256,1024]{1,0:T(8,128)(2,1)S(1)}, bf16[256,1024]{1,0:T(8,128)(2,1)S(1)}, u32[]{:S(2)}, u32[]{:S(2)}) collective-permute-start(bf16[256,1024]{1,0:T(8,128)(2,1)S(1)} %slice.6), channel_id=1, source_target_pairs={{0,1},{1,2},{2,3},{3,0},{4,5},{5,6},{6,7},{7,4},{8,9},{9,10},{10,1... | collective-permute-start | bytes 1572872 | tf_op jit(solution)/shard_map/ppermute | solution.py:42
  77.9 8.1 %collective-permute-start.10 = (bf16[256,1024]{1,0:T(8,128)(2,1)}, bf16[256,1024]{1,0:T(8,128)(2,1)S(1)}, u32[]{:S(2)}, u32[]{:S(2)}) collective-permute-start(bf16[256,1024]{1,0:T(8,128)(2,1)} %collective-permute-done.8.refs_4_), channel_id=1, source_target_pairs={{0,16},{1,17},{2,18},{3,19},{4,20},{5,21},{6,22},{7,23},{8,24},{9,... | collective-permute-start | bytes 1572872 | tf_op jit(solution)/shard_map/ppermute | solution.py:42
  81.4 6.4 %copy-start.5 = (bf16[256,1024]{1,0:T(8,128)(2,1)}, bf16[256,1024]{1,0:T(8,128)(2,1)S(1)}, u32[]{:S(2)}) copy-start(bf16[256,1024]{1,0:T(8,128)(2,1)S(1)} %collective-permute-done.7.refs_3_) | copy-start | bytes 1572868
  81.4 5.5 %collective-permute-start.9 = (bf16[256,1024]{1,0:T(8,128)(2,1)S(1)}, bf16[256,1024]{1,0:T(8,128)(2,1)}, u32[]{:S(2)}, u32[]{:S(2)}) collective-permute-start(bf16[256,1024]{1,0:T(8,128)(2,1)S(1)} %collective-permute-done.7.refs_3_), channel_id=1, source_target_pairs={{0,16},{1,17},{2,18},{3,19},{4,20},{5,21},{6,22},{7,23},{8,24},{9,... | collective-permute-start | bytes 1572872 | tf_op jit(solution)/shard_map/ppermute | solution.py:42
  86.0 1.8 %copy-start.6 = (bf16[256,1024]{1,0:T(8,128)(2,1)}, bf16[256,1024]{1,0:T(8,128)(2,1)S(1)}, u32[]{:S(2)}) copy-start(bf16[256,1024]{1,0:T(8,128)(2,1)S(1)} %collective-permute-done.10.refs_9_) | copy-start | bytes 1572868
  87.8 1.3 copy-start
  96.5 57.6 %copy-start.7 = (f32[128,128]{1,0:T(8,128)S(1)}, f32[128,128]{1,0:T(8,128)}, u32[]{:S(2)}) copy-start(f32[128,128]{1,0:T(8,128)} %param.7) | copy-start | bytes 196612
  96.5 16.0 %collective-permute-start.12 = (bf16[512,128]{1,0:T(8,128)(2,1)S(1)}, bf16[512,128]{1,0:T(8,128)(2,1)S(1)}, u32[]{:S(2)}, u32[]{:S(2)}) collective-permute-start(bf16[512,128]{1,0:T(8,128)(2,1)S(1)} %get-tuple-element.24), channel_id=1, source_target_pairs={{4,20},{5,21},{6,22},{7,23},{8,4},{9,5},{10,6},{11,7},{12,8},{13,9... | collective-permute-start | bytes 393224 | tf_op jit(solution)/shard_map/ppermute | solution.py:42
  104.5 8.0 %collective-permute-start.13 = (bf16[512,128]{1,0:T(8,128)(2,1)S(1)}, bf16[512,128]{1,0:T(8,128)(2,1)S(1)}, u32[]{:S(2)}, u32[]{:S(2)}) collective-permute-start(bf16[512,128]{1,0:T(8,128)(2,1)S(1)} %get-tuple-element.23), channel_id=1, source_target_pairs={{0,16},{1,17},{2,18},{3,19},{8,12},{9,13},{10,14},{11,15},{12,0},{... | collective-permute-start | bytes 393224 | tf_op jit(solution)/shard_map/ppermute | solution.py:42
  106.4 15.6 %collective-permute-start.11 = (bf16[512,128]{1,0:T(8,128)(2,1)S(1)}, bf16[512,128]{1,0:T(8,128)(2,1)S(1)}, u32[]{:S(2)}, u32[]{:S(2)}) collective-permute-start(bf16[512,128]{1,0:T(8,128)(2,1)S(1)} %get-tuple-element.22), channel_id=1, source_target_pairs={{0,20},{1,21},{2,22},{3,23},{4,0},{5,1},{6,2},{7,3},{8,4},{9,5},{1... | collective-permute-start | bytes 393224 | tf_op jit(solution)/shard_map/ppermute | solution.py:42
  113.5 10.4 %collective-permute-start.14 = (bf16[512,128]{1,0:T(8,128)(2,1)S(1)}, bf16[512,128]{1,0:T(8,128)(2,1)S(1)}, u32[]{:S(2)}, u32[]{:S(2)}) collective-permute-start(bf16[512,128]{1,0:T(8,128)(2,1)S(1)} %fusion), channel_id=1, source_target_pairs={{0,4},{1,5},{2,6},{3,7},{4,16},{5,17},{6,18},{7,19},{8,20},{9,21},... | collective-permute-start | bytes 393224 | tf_op jit(solution)/shard_map/ppermute | solution.py:42

commit v4 on v3

--- a/solution.py
+++ b/solution.py
@@ -149,7 +149,6 @@
     )
     expanded = jnp.broadcast_to(local_mask[:, :, None], (row_blocks, W, W)).reshape(rows, W)
     masked = factor_panel * expanded.astype(BF)
-    ancestor_inverse, masked = lax.optimization_barrier((ancestor_inverse, masked))
     half = rows // 2
     before = send(ancestor_inverse, along_x(1))
     after = send(ancestor_inverse, along_x(3))
@@ -157,10 +156,11 @@
     block, before, after = lax.optimization_barrier((block, before, after))
     near = gather(block, "prow", ZLO)
     swapped = [send(part, swap) for part in (ancestor_inverse, before, after)]
-    near, *swapped = lax.optimization_barrier((near, *swapped))
+    top, bottom = before[:half], after[half:]
+    near, top, bottom, *swapped = lax.optimization_barrier((near, top, bottom, *swapped))
     panel = gather(near, "prow", Y).reshape(4, 2, 2 * rows, W)
-    top = send(before[:half], along_x(1))
-    bottom = send(after[half:], along_x(3))
+    top = send(top, along_x(1))
+    bottom = send(bottom, along_x(3))
     ours = [ancestor_inverse, before, after, top, bottom]
     others = swapped + [send(part, swap) for part in ours[3:]]
     stays = core == z_hi // 2

time: 156 us -> 153 us (0.981)
  waiting for transfers between devices: 25.6 us -> 41.3 us
  blocking collectives: 28 us -> 16.8 us
  starting transfers between devices: 79.4 us -> 71.4 us
    ppermute x15, waiting for transfers between devices: 20.9 us -> 33.4 us  [send(): return lax.ppermute(block, BOTH, moves(to))]
    all_to_all x2, blocking collectives: 28 us -> 16.8 us  [gather(): return lax.all_to_all(copies, axis, 0, 0, axis_index_groups=members)]
    ppermute x15, starting transfers between devices: 63.9 us -> 58.4 us  [send(): return lax.ppermute(block, BOTH, moves(to))]
    all_to_all x2, waiting for transfers between devices: 4.67 us -> 7.93 us  [gather(): return lax.all_to_all(copies, axis, 0, 0, axis_index_groups=members)]
    all_to_all x2, starting transfers between devices: 15.4 us -> 12.9 us  [gather(): return lax.all_to_all(copies, axis, 0, 0, axis_index_groups=members)]
  transfers between devices with their start and end apart: 17 -> 17, of which waited for: 9 -> 7; matrix products, arithmetic and copies ran while one was open for 2% -> 3% of each run, Pallas kernels for 0% -> 0%
where the time goes in v4:
time: 153 us; the launch traced here: 152 us
  starting transfers between devices  71.4 us (47%)
  waiting for transfers between devices  41.3 us (27%)
  blocking collectives  16.8 us (11%)
  local copies, waits for them, and re-layouts  9.69 us (6%)
  Pallas kernels  6.3 us (4%)
  other arithmetic  5.22 us (3%)
    ppermute x15, starting transfers between devices, send(): return lax.ppermute(block, BOTH, moves(to))  58.4 us
    ppermute x15, waiting for transfers between devices, send(): return lax.ppermute(block, BOTH, moves(to))  33.4 us
    all_to_all x2, blocking collectives, gather(): return lax.all_to_all(copies, axis, 0, 0, axis_index_groups=members)  16.8 us
    all_to_all x2, starting transfers between devices, gather(): return lax.all_to_all(copies, axis, 0, 0, axis_index_groups=members)  12.9 us
    all_to_all x2, waiting for transfers between devices, gather(): return lax.all_to_all(copies, axis, 0, 0, axis_index_groups=members)  7.93 us
    pallas_call x1, Pallas kernels, times(): pl.pallas_call(times_kernel, in_specs=[pl.BlockSpec(memory_space=pltpu.SM...  6.3 us
    unnamed x16, local copies, waits for them, and re-layouts  3.3 us
  transfers between devices with their start and end apart: 17, of which 7 were waited for; matrix products, arithmetic and copies ran while one was open for 3% of the time, Pallas kernels for 0%

profile of v4, /device:TPU:1, one launch (start us, length us, event | category | flops | bytes accessed | tf_op | source)
XLA Modules:
  0.0 152.0 jit_solution(9967532195978121453)
XLA Ops:
  0.6 4.0 %collective-permute-start.2 = (bf16[512,1024]{1,0:T(8,128)(2,1)}, bf16[512,1024]{1,0:T(8,128)(2,1)S(1)}, u32[]{:S(2)}, u32[]{:S(2)}) collective-permute-start(bf16[512,1024]{1,0:T(8,128)(2,1)} %refs_0_.1), channel_id=1, source_target_pairs={{0,1},{1,2},{2,3},{3,0},{4,5},{5,6},{6,7},{7,4},{8,9},{9,10},{10,1... | collective-permute-start | bytes 3145736 | tf_op jit(solution)/shard_map/ppermute | solution.py:42
  4.6 3.2 %collective-permute-start.3 = (bf16[512,1024]{1,0:T(8,128)(2,1)}, bf16[512,1024]{1,0:T(8,128)(2,1)S(1)}, u32[]{:S(2)}, u32[]{:S(2)}) collective-permute-start(bf16[512,1024]{1,0:T(8,128)(2,1)} %refs_0_.1), channel_id=1, source_target_pairs={{0,3},{1,0},{2,1},{3,2},{4,7},{5,4},{6,5},{7,6},{8,11},{9,8},{10,9... | collective-permute-start | bytes 3145736 | tf_op jit(solution)/shard_map/ppermute | solution.py:42
  7.8 0.8 convert_bitcast_fusion
  8.6 0.1 broadcast_bitcast_fusion.1
  8.6 1.0 broadcast_multiply_fusion
  9.7 0.7 collective-permute-start
  10.4 12.2 %collective-permute-start.1 = (bf16[512,128]{1,0:T(8,128)(2,1)S(1)}, bf16[512,128]{1,0:T(8,128)(2,1)S(1)}, u32[]{:S(2)}, u32[]{:S(2)}) collective-permute-start(bf16[512,128]{1,0:T(8,128)(2,1)S(1)} %collective-permute-done), channel_id=1, source_target_pairs={{0,0},{1,1},{2,2},{3,3},{4,64},{5,65},{6,66},{7,67},{8,16},{9,17},... | collective-permute-start | bytes 393224 | tf_op jit(solution)/shard_map/ppermute | solution.py:42
  22.6 7.3 %collective-permute-done.1 = bf16[512,128]{1,0:T(8,128)(2,1)S(1)} collective-permute-done((bf16[512,128]{1,0:T(8,128)(2,1)S(1)}, bf16[512,128]{1,0:T(8,128)(2,1)S(1)}, u32[]{:S(2)}, u32[]{:S(2)}) %collective-permute-start.1) | collective-permute-done | bytes 131104 | tf_op jit(solution)/shard_map/ppermute | solution.py:42
  29.9 0.0 collective-permute-done.3.refs_2_
  29.9 1.0 broadcast_in_dim.18
  30.8 8.6 %all-to-all-start = ((bf16[4,512,128]{2,1,0:T(8,128)(2,1)}), bf16[4,512,128]{2,1,0:T(8,128)(2,1)S(1)}, u32[]{:S(2)}, u32[]{:S(2)}) async-start(bf16[4,512,128]{2,1,0:T(8,128)(2,1)} %broadcast_in_dim.18), calls=%async_computation | async-start | bytes 1048576 | tf_op jit(solution)/shard_map/all_to_all | solution.py:84
  39.4 1.9 %collective-permute-start.4 = (bf16[512,1024]{1,0:T(8,128)(2,1)}, bf16[512,1024]{1,0:T(8,128)(2,1)S(1)}, u32[]{:S(2)}, u32[]{:S(2)}) collective-permute-start(bf16[512,1024]{1,0:T(8,128)(2,1)} %refs_0_.1), channel_id=1, source_target_pairs={{0,16},{1,17},{2,18},{3,19},{4,20},{5,21},{6,22},{7,23},{8,24},{9,... | collective-permute-start | bytes 3145736 | tf_op jit(solution)/shard_map/ppermute | solution.py:42
  41.3 2.4 %collective-permute-start.5 = (bf16[512,1024]{1,0:T(8,128)(2,1)S(1)}, bf16[512,1024]{1,0:T(8,128)(2,1)S(1)}, u32[]{:S(2)}, u32[]{:S(2)}) collective-permute-start(bf16[512,1024]{1,0:T(8,128)(2,1)S(1)} %collective-permute-done.2.refs_1_), channel_id=1, source_target_pairs={{0,16},{1,17},{2,18},{3,19},{4,20},{5,21},{6,22},{7,23},{8,24},{9,... | collective-permute-start | bytes 3145736 | tf_op jit(solution)/shard_map/ppermute | solution.py:42
  43.7 1.9 %collective-permute-start.6 = (bf16[512,1024]{1,0:T(8,128)(2,1)S(1)}, bf16[512,1024]{1,0:T(8,128)(2,1)}, u32[]{:S(2)}, u32[]{:S(2)}) collective-permute-start(bf16[512,1024]{1,0:T(8,128)(2,1)S(1)} %collective-permute-done.3.refs_2_), channel_id=1, source_target_pairs={{0,16},{1,17},{2,18},{3,19},{4,20},{5,21},{6,22},{7,23},{8,24},{9,... | collective-permute-start | bytes 3145736 | tf_op jit(solution)/shard_map/ppermute | solution.py:42
  45.7 0.9 slice.6
  46.6 0.9 slice.7
  47.5 0.0 collective-permute-done.4.refs_5_
  47.5 1.0 copy-done.3
  48.4 1.0 copy-done.4
  49.4 0.0 collective-permute-done.6.refs_7_
  49.4 4.9 %all-to-all-done = bf16[4,512,128]{2,1,0:T(8,128)(2,1)S(1)} async-done(((bf16[4,512,128]{2,1,0:T(8,128)(2,1)}), bf16[4,512,128]{2,1,0:T(8,128)(2,1)S(1)}, u32[]{:S(2)}, u32[]{:S(2)}) %all-to-all-start) | async-done | bytes 524320 | tf_op jit(solution)/shard_map/all_to_all | solution.py:84
  54.3 1.8 %broadcast_in_dim.19 = bf16[4,4,512,128]{3,2,1,0:T(8,128)(2,1)} broadcast(bf16[4,512,128]{2,1,0:T(8,128)(2,1)S(1)} %all-to-all-done), dimensions={1,2,3} | broadcast | bytes 2621440 | tf_op jit(solution)/shard_map/broadcast_in_dim | solution.py:83
  56.1 4.4 %all-to-all-start.1 = ((bf16[4,4,512,128]{3,2,1,0:T(8,128)(2,1)}), bf16[4,4,512,128]{3,2,1,0:T(8,128)(2,1)S(1)}, u32[]{:S(2)}, u32[]{:S(2)}) async-start(bf16[4,4,512,128]{3,2,1,0:T(8,128)(2,1)} %broadcast_in_dim.19), calls=%async_computation.1 | async-start | bytes 4194304 | tf_op jit(solution)/shard_map/all_to_all | solution.py:84
  60.5 2.9 %collective-permute-start.7 = (bf16[256,1024]{1,0:T(8,128)(2,1)}, bf16[256,1024]{1,0:T(8,128)(2,1)S(1)}, u32[]{:S(2)}, u32[]{:S(2)}) collective-permute-start(bf16[256,1024]{1,0:T(8,128)(2,1)} %slice.6), channel_id=1, source_target_pairs={{0,1},{1,2},{2,3},{3,0},{4,5},{5,6},{6,7},{7,4},{8,9},{9,10},{10,1... | collective-permute-start | bytes 1572872 | tf_op jit(solution)/shard_map/ppermute | solution.py:42
  63.4 3.7 %collective-permute-start.8 = (bf16[256,1024]{1,0:T(8,128)(2,1)}, bf16[256,1024]{1,0:T(8,128)(2,1)S(1)}, u32[]{:S(2)}, u32[]{:S(2)}) collective-permute-start(bf16[256,1024]{1,0:T(8,128)(2,1)} %slice.7), channel_id=1, source_target_pairs={{0,3},{1,0},{2,1},{3,2},{4,7},{5,4},{6,5},{7,6},{8,11},{9,8},{10,9... | collective-permute-start | bytes 1572872 | tf_op jit(solution)/shard_map/ppermute | solution.py:42
  67.1 9.9 %collective-permute-done.7.refs_3_ = bf16[256,1024]{1,0:T(8,128)(2,1)S(1)} collective-permute-done((bf16[256,1024]{1,0:T(8,128)(2,1)}, bf16[256,1024]{1,0:T(8,128)(2,1)S(1)}, u32[]{:S(2)}, u32[]{:S(2)}) %collective-permute-start.7) | collective-permute-done | bytes 524320 | tf_op jit(solution)/shard_map/ppermute | solution.py:42
  77.0 3.1 %collective-permute-start.9 = (bf16[256,1024]{1,0:T(8,128)(2,1)S(1)}, bf16[256,1024]{1,0:T(8,128)(2,1)}, u32[]{:S(2)}, u32[]{:S(2)}) collective-permute-start(bf16[256,1024]{1,0:T(8,128)(2,1)S(1)} %collective-permute-done.7.refs_3_), channel_id=1, source_target_pairs={{0,16},{1,17},{2,18},{3,19},{4,20},{5,21},{6,22},{7,23},{8,24},{9,... | collective-permute-start | bytes 1572872 | tf_op jit(solution)/shard_map/ppermute | solution.py:42
  80.1 1.9 %collective-permute-start.10 = (bf16[256,1024]{1,0:T(8,128)(2,1)S(1)}, bf16[256,1024]{1,0:T(8,128)(2,1)}, u32[]{:S(2)}, u32[]{:S(2)}) collective-permute-start(bf16[256,1024]{1,0:T(8,128)(2,1)S(1)} %collective-permute-done.8.refs_4_), channel_id=1, source_target_pairs={{0,16},{1,17},{2,18},{3,19},{4,20},{5,21},{6,22},{7,23},{8,24},{9,... | collective-permute-start | bytes 1572872 | tf_op jit(solution)/shard_map/ppermute | solution.py:42
  82.2 0.6 stack.31.order
  82.9 1.2 collective-permute-done.10.refs_9_
  84.1 3.0 %all-to-all-done.1 = bf16[4,4,512,128]{3,2,1,0:T(8,128)(2,1)S(1)} async-done(((bf16[4,4,512,128]{3,2,1,0:T(8,128)(2,1)}), bf16[4,4,512,128]{3,2,1,0:T(8,128)(2,1)S(1)}, u32[]{:S(2)}, u32[]{:S(2)}) %all-to-all-start.1) | async-done | bytes 2097184 | tf_op jit(solution)/shard_map/all_to_all | solution.py:84
  87.1 1.3 copy-done
  88.4 6.3 %shard_map.59 = bf16[4,512,128]{2,1,0:T(8,128)(2,1)} custom-call(s32[7]{0:T(128)} %stack.31.order, bf16[4,2,1024,128]{3,2,1,0:T(8,128)(2,1)} %bitcast.34, bf16[512,1024]{1,0:T(8,128)(2,1)} %refs_0_.1, bf16[512,1024]{1,0:T(8,128)(2,1)} %copy-done.1, bf16[512,1024]{1,0:T(8,128)(2,1)} %copy-done.2, bf16[256,1024]{1,0:T(8,128)(2,1)} %copy-done.5, ...), custom_call_target="tpu_custom_call" | custom-call | flops 2147483648 | bytes 9437184 | tf_op jit(solution)/shard_map/pallas_call | solution.py:122
  94.7 1.1 slice_bitcast_fusion.3
  95.8 0.0 copy-start.7
  95.8 5.1 %collective-permute-start.13 = (bf16[512,128]{1,0:T(8,128)(2,1)S(1)}, bf16[512,128]{1,0:T(8,128)(2,1)S(1)}, u32[]{:S(2)}, u32[]{:S(2)}) collective-permute-start(bf16[512,128]{1,0:T(8,128)(2,1)S(1)} %get-tuple-element.23), channel_id=1, source_target_pairs={{0,16},{1,17},{2,18},{3,19},{8,12},{9,13},{10,14},{11,15},{12,0},{... | collective-permute-start | bytes 393224 | tf_op jit(solution)/shard_map/ppermute | solution.py:42
  100.9 3.1 %collective-permute-start.12 = (bf16[512,128]{1,0:T(8,128)(2,1)S(1)}, bf16[512,128]{1,0:T(8,128)(2,1)S(1)}, u32[]{:S(2)}, u32[]{:S(2)}) collective-permute-start(bf16[512,128]{1,0:T(8,128)(2,1)S(1)} %get-tuple-element.24), channel_id=1, source_target_pairs={{4,20},{5,21},{6,22},{7,23},{8,4},{9,5},{10,6},{11,7},{12,8},{13,9... | collective-permute-start | bytes 393224 | tf_op jit(solution)/shard_map/ppermute | solution.py:42
  104.1 10.4 %collective-permute-start.11 = (bf16[512,128]{1,0:T(8,128)(2,1)S(1)}, bf16[512,128]{1,0:T(8,128)(2,1)S(1)}, u32[]{:S(2)}, u32[]{:S(2)}) collective-permute-start(bf16[512,128]{1,0:T(8,128)(2,1)S(1)} %get-tuple-element.22), channel_id=1, source_target_pairs={{0,20},{1,21},{2,22},{3,23},{4,0},{5,1},{6,2},{7,3},{8,4},{9,5},{1... | collective-permute-start | bytes 393224 | tf_op jit(solution)/shard_map/ppermute | solution.py:42
  114.5 4.6 %collective-permute-done.12 = bf16[512,128]{1,0:T(8,128)(2,1)S(1)} collective-permute-done((bf16[512,128]{1,0:T(8,128)(2,1)S(1)}, bf16[512,128]{1,0:T(8,128)(2,1)S(1)}, u32[]{:S(2)}, u32[]{:S(2)}) %collective-permute-start.12) | collective-permute-done | bytes 131104 | tf_op jit(solution)/shard_map/ppermute | solution.py:42
  119.1 1.0 fusion
  120.0 1.9 %collective-permute-start.14 = (bf16[512,128]{1,0:T(8,128)(2,1)S(1)}, bf16[512,128]{1,0:T(8,128)(2,1)S(1)}, u32[]{:S(2)}, u32[]{:S(2)}) collective-permute-start(bf16[512,128]{1,0:T(8,128)(2,1)S(1)} %fusion), channel_id=1, source_target_pairs={{0,4},{1,5},{2,6},{3,7},{4,16},{5,17},{6,18},{7,19},{8,20},{9,21},... | collective-permute-start | bytes 393224 | tf_op jit(solution)/shard_map/ppermute | solution.py:42
  122.0 0.1 broadcast_bitcast_fusion
  122.0 10.4 %collective-permute-done.14 = bf16[512,128]{1,0:T(8,128)(2,1)S(1)} collective-permute-done((bf16[512,128]{1,0:T(8,128)(2,1)S(1)}, bf16[512,128]{1,0:T(8,128)(2,1)S(1)}, u32[]{:S(2)}, u32[]{:S(2)}) %collective-permute-start.14) | collective-permute-done | bytes 131104 | tf_op jit(solution)/shard_map/ppermute | solution.py:42
  132.4 1.8 %multiply_convert_fusion = (bf16[512,128]{1,0:T(8,128)(2,1)}, bf16[512,128]{1,0:T(8,128)(2,1)S(1)}) fusion(bf16[512,128]{1,0:T(8,128)(2,1)S(1)} %collective-permute-done.14, bf16[512,128]{1,0:T(8,128)(2,1)S(1)} %collective-permute-done.11, f32[512]{0:T(512)S(1)} %broadcast_bitcast_fusion, bf16[512,128]{1,0:T(8,128)(2,1)S(1)} %collective-permute-done.12, ...), kind=kLoop, calls=%fused_computation.4 | loop fusion | flops 720896 | bytes 1050627 | tf_op jit(solution)/shard_map/convert_element_type | solution.py:179
  134.2 0.2 convolution_convert_fusion
  134.5 9.6 %all_to_all.20 = bf16[8,128,128]{2,1,0:T(8,128)(2,1)S(1)} all-to-all(bf16[8,128,128]{2,1,0:T(8,128)(2,1)S(1)} %broadcast_in_dim.42), channel_id=1, replica_groups={{0,16,128,144,256,272,384,400},{32,48,160,176,288,304,416,432},{64,80,1..., dimensions={0} | all-to-all | bytes 524288 | tf_op jit(solution)/shard_map/all_to_all | solution.py:84
  144.1 7.2 %all_to_all.21 = bf16[4,128,128]{2,1,0:T(8,128)(2,1)S(1)} all-to-all(bf16[4,128,128]{2,1,0:T(8,128)(2,1)S(1)} %broadcast_in_dim.43), channel_id=1, replica_groups={{0,32,64,96},{16,48,80,112},{128,160,192,224},{144,176,208,240},{256,28..., dimensions={0} | all-to-all | bytes 262144 | tf_op jit(solution)/shard_map/all_to_all | solution.py:84
  151.4 0.6 add.88
  (23 shorter events, 0.2 us)
Async XLA Ops:
  0.6 29.2 %collective-permute-start.2 = (bf16[512,1024]{1,0:T(8,128)(2,1)}, bf16[512,1024]{1,0:T(8,128)(2,1)S(1)}, u32[]{:S(2)}, u32[]{:S(2)}) collective-permute-start(bf16[512,1024]{1,0:T(8,128)(2,1)} %refs_0_.1), channel_id=1, source_target_pairs={{0,1},{1,2},{2,3},{3,0},{4,5},{5,6},{6,7},{7,4},{8,9},{9,10},{10,1... | collective-permute-start | bytes 3145736 | tf_op jit(solution)/shard_map/ppermute | solution.py:42
  4.6 25.3 %collective-permute-start.3 = (bf16[512,1024]{1,0:T(8,128)(2,1)}, bf16[512,1024]{1,0:T(8,128)(2,1)S(1)}, u32[]{:S(2)}, u32[]{:S(2)}) collective-permute-start(bf16[512,1024]{1,0:T(8,128)(2,1)} %refs_0_.1), channel_id=1, source_target_pairs={{0,3},{1,0},{2,1},{3,2},{4,7},{5,4},{6,5},{7,6},{8,11},{9,8},{10,9... | collective-permute-start | bytes 3145736 | tf_op jit(solution)/shard_map/ppermute | solution.py:42
  9.7 0.7 collective-permute-start
  10.4 19.5 %collective-permute-start.1 = (bf16[512,128]{1,0:T(8,128)(2,1)S(1)}, bf16[512,128]{1,0:T(8,128)(2,1)S(1)}, u32[]{:S(2)}, u32[]{:S(2)}) collective-permute-start(bf16[512,128]{1,0:T(8,128)(2,1)S(1)} %collective-permute-done), channel_id=1, source_target_pairs={{0,0},{1,1},{2,2},{3,3},{4,64},{5,65},{6,66},{7,67},{8,16},{9,17},... | collective-permute-start | bytes 393224 | tf_op jit(solution)/shard_map/ppermute | solution.py:42
  29.9 26.2 %copy-start.1 = (bf16[512,1024]{1,0:T(8,128)(2,1)}, bf16[512,1024]{1,0:T(8,128)(2,1)S(1)}, u32[]{:S(2)}) copy-start(bf16[512,1024]{1,0:T(8,128)(2,1)S(1)} %collective-permute-done.2.refs_1_) | copy-start | bytes 3145732
  29.9 26.2 %copy-start.2 = (bf16[512,1024]{1,0:T(8,128)(2,1)}, bf16[512,1024]{1,0:T(8,128)(2,1)S(1)}, u32[]{:S(2)}) copy-start(bf16[512,1024]{1,0:T(8,128)(2,1)S(1)} %collective-permute-done.3.refs_2_) | copy-start | bytes 3145732
  30.8 23.5 %all-to-all-start = ((bf16[4,512,128]{2,1,0:T(8,128)(2,1)}), bf16[4,512,128]{2,1,0:T(8,128)(2,1)S(1)}, u32[]{:S(2)}, u32[]{:S(2)}) async-start(bf16[4,512,128]{2,1,0:T(8,128)(2,1)} %broadcast_in_dim.18), calls=%async_computation | async-start | bytes 1048576 | tf_op jit(solution)/shard_map/all_to_all | solution.py:84
  39.4 8.0 %collective-permute-start.4 = (bf16[512,1024]{1,0:T(8,128)(2,1)}, bf16[512,1024]{1,0:T(8,128)(2,1)S(1)}, u32[]{:S(2)}, u32[]{:S(2)}) collective-permute-start(bf16[512,1024]{1,0:T(8,128)(2,1)} %refs_0_.1), channel_id=1, source_target_pairs={{0,16},{1,17},{2,18},{3,19},{4,20},{5,21},{6,22},{7,23},{8,24},{9,... | collective-permute-start | bytes 3145736 | tf_op jit(solution)/shard_map/ppermute | solution.py:42
  41.3 6.1 %collective-permute-start.5 = (bf16[512,1024]{1,0:T(8,128)(2,1)S(1)}, bf16[512,1024]{1,0:T(8,128)(2,1)S(1)}, u32[]{:S(2)}, u32[]{:S(2)}) collective-permute-start(bf16[512,1024]{1,0:T(8,128)(2,1)S(1)} %collective-permute-done.2.refs_1_), channel_id=1, source_target_pairs={{0,16},{1,17},{2,18},{3,19},{4,20},{5,21},{6,22},{7,23},{8,24},{9,... | collective-permute-start | bytes 3145736 | tf_op jit(solution)/shard_map/ppermute | solution.py:42
  43.7 5.7 %collective-permute-start.6 = (bf16[512,1024]{1,0:T(8,128)(2,1)S(1)}, bf16[512,1024]{1,0:T(8,128)(2,1)}, u32[]{:S(2)}, u32[]{:S(2)}) collective-permute-start(bf16[512,1024]{1,0:T(8,128)(2,1)S(1)} %collective-permute-done.3.refs_2_), channel_id=1, source_target_pairs={{0,16},{1,17},{2,18},{3,19},{4,20},{5,21},{6,22},{7,23},{8,24},{9,... | collective-permute-start | bytes 3145736 | tf_op jit(solution)/shard_map/ppermute | solution.py:42
  47.5 1.0 copy-start.3
  48.4 1.0 copy-start.4
  56.1 31.0 %all-to-all-start.1 = ((bf16[4,4,512,128]{3,2,1,0:T(8,128)(2,1)}), bf16[4,4,512,128]{3,2,1,0:T(8,128)(2,1)S(1)}, u32[]{:S(2)}, u32[]{:S(2)}) async-start(bf16[4,4,512,128]{3,2,1,0:T(8,128)(2,1)} %broadcast_in_dim.19), calls=%async_computation.1 | async-start | bytes 4194304 | tf_op jit(solution)/shard_map/all_to_all | solution.py:84
  60.5 16.5 %collective-permute-start.7 = (bf16[256,1024]{1,0:T(8,128)(2,1)}, bf16[256,1024]{1,0:T(8,128)(2,1)S(1)}, u32[]{:S(2)}, u32[]{:S(2)}) collective-permute-start(bf16[256,1024]{1,0:T(8,128)(2,1)} %slice.6), channel_id=1, source_target_pairs={{0,1},{1,2},{2,3},{3,0},{4,5},{5,6},{6,7},{7,4},{8,9},{9,10},{10,1... | collective-permute-start | bytes 1572872 | tf_op jit(solution)/shard_map/ppermute | solution.py:42
  63.4 16.7 %collective-permute-start.8 = (bf16[256,1024]{1,0:T(8,128)(2,1)}, bf16[256,1024]{1,0:T(8,128)(2,1)S(1)}, u32[]{:S(2)}, u32[]{:S(2)}) collective-permute-start(bf16[256,1024]{1,0:T(8,128)(2,1)} %slice.7), channel_id=1, source_target_pairs={{0,3},{1,0},{2,1},{3,2},{4,7},{5,4},{6,5},{7,6},{8,11},{9,8},{10,9... | collective-permute-start | bytes 1572872 | tf_op jit(solution)/shard_map/ppermute | solution.py:42
  77.0 10.1 %copy-start.5 = (bf16[256,1024]{1,0:T(8,128)(2,1)}, bf16[256,1024]{1,0:T(8,128)(2,1)S(1)}, u32[]{:S(2)}) copy-start(bf16[256,1024]{1,0:T(8,128)(2,1)S(1)} %collective-permute-done.7.refs_3_) | copy-start | bytes 1572868
  77.0 5.9 %collective-permute-start.9 = (bf16[256,1024]{1,0:T(8,128)(2,1)S(1)}, bf16[256,1024]{1,0:T(8,128)(2,1)}, u32[]{:S(2)}, u32[]{:S(2)}) collective-permute-start(bf16[256,1024]{1,0:T(8,128)(2,1)S(1)} %collective-permute-done.7.refs_3_), channel_id=1, source_target_pairs={{0,16},{1,17},{2,18},{3,19},{4,20},{5,21},{6,22},{7,23},{8,24},{9,... | collective-permute-start | bytes 1572872 | tf_op jit(solution)/shard_map/ppermute | solution.py:42
  80.1 7.0 %copy-start.6 = (bf16[256,1024]{1,0:T(8,128)(2,1)}, bf16[256,1024]{1,0:T(8,128)(2,1)S(1)}, u32[]{:S(2)}) copy-start(bf16[256,1024]{1,0:T(8,128)(2,1)S(1)} %collective-permute-done.8.refs_4_) | copy-start | bytes 1572868
  80.1 3.9 %collective-permute-start.10 = (bf16[256,1024]{1,0:T(8,128)(2,1)S(1)}, bf16[256,1024]{1,0:T(8,128)(2,1)}, u32[]{:S(2)}, u32[]{:S(2)}) collective-permute-start(bf16[256,1024]{1,0:T(8,128)(2,1)S(1)} %collective-permute-done.8.refs_4_), channel_id=1, source_target_pairs={{0,16},{1,17},{2,18},{3,19},{4,20},{5,21},{6,22},{7,23},{8,24},{9,... | collective-permute-start | bytes 1572872 | tf_op jit(solution)/shard_map/ppermute | solution.py:42
  87.1 1.3 copy-start
  95.8 55.6 %copy-start.7 = (f32[128,128]{1,0:T(8,128)S(1)}, f32[128,128]{1,0:T(8,128)}, u32[]{:S(2)}) copy-start(f32[128,128]{1,0:T(8,128)} %param.7) | copy-start | bytes 196612
  95.8 18.7 %collective-permute-start.13 = (bf16[512,128]{1,0:T(8,128)(2,1)S(1)}, bf16[512,128]{1,0:T(8,128)(2,1)S(1)}, u32[]{:S(2)}, u32[]{:S(2)}) collective-permute-start(bf16[512,128]{1,0:T(8,128)(2,1)S(1)} %get-tuple-element.23), channel_id=1, source_target_pairs={{0,16},{1,17},{2,18},{3,19},{8,12},{9,13},{10,14},{11,15},{12,0},{... | collective-permute-start | bytes 393224 | tf_op jit(solution)/shard_map/ppermute | solution.py:42
  100.9 18.1 %collective-permute-start.12 = (bf16[512,128]{1,0:T(8,128)(2,1)S(1)}, bf16[512,128]{1,0:T(8,128)(2,1)S(1)}, u32[]{:S(2)}, u32[]{:S(2)}) collective-permute-start(bf16[512,128]{1,0:T(8,128)(2,1)S(1)} %get-tuple-element.24), channel_id=1, source_target_pairs={{4,20},{5,21},{6,22},{7,23},{8,4},{9,5},{10,6},{11,7},{12,8},{13,9... | collective-permute-start | bytes 393224 | tf_op jit(solution)/shard_map/ppermute | solution.py:42
  104.1 18.0 %collective-permute-start.11 = (bf16[512,128]{1,0:T(8,128)(2,1)S(1)}, bf16[512,128]{1,0:T(8,128)(2,1)S(1)}, u32[]{:S(2)}, u32[]{:S(2)}) collective-permute-start(bf16[512,128]{1,0:T(8,128)(2,1)S(1)} %get-tuple-element.22), channel_id=1, source_target_pairs={{0,20},{1,21},{2,22},{3,23},{4,0},{5,1},{6,2},{7,3},{8,4},{9,5},{1... | collective-permute-start | bytes 393224 | tf_op jit(solution)/shard_map/ppermute | solution.py:42
  120.0 12.4 %collective-permute-start.14 = (bf16[512,128]{1,0:T(8,128)(2,1)S(1)}, bf16[512,128]{1,0:T(8,128)(2,1)S(1)}, u32[]{:S(2)}, u32[]{:S(2)}) collective-permute-start(bf16[512,128]{1,0:T(8,128)(2,1)S(1)} %fusion), channel_id=1, source_target_pairs={{0,4},{1,5},{2,6},{3,7},{4,16},{5,17},{6,18},{7,19},{8,20},{9,21},... | collective-permute-start | bytes 393224 | tf_op jit(solution)/shard_map/ppermute | solution.py:42

commit v5 on v4

--- a/solution.py
+++ b/solution.py
@@ -144,16 +144,21 @@
     z_hi, x = col_index // 4, col_index % 4
     rows = factor_panel.shape[0]
     row_blocks = rows // W
-    local_mask = lax.dynamic_slice(
-        pattern, (row_index * row_blocks, col_index), (row_blocks, 1)
-    )
-    expanded = jnp.broadcast_to(local_mask[:, :, None], (row_blocks, W, W)).reshape(rows, W)
+
+    def mask_of(r, c):
+        mask = lax.dynamic_slice(pattern, (r * row_blocks, c), (row_blocks, 1))
+        return jnp.broadcast_to(mask[:, :, None], (row_blocks, W, W)).reshape(rows, W)
+
+    expanded = mask_of(row_index, col_index)
     masked = factor_panel * expanded.astype(BF)
     half = rows // 2
     before = send(ancestor_inverse, along_x(1))
     after = send(ancestor_inverse, along_x(3))
-    block = send(send(masked, spread_y), spread_z)
+    block = send(send(factor_panel, spread_y), spread_z)
     block, before, after = lax.optimization_barrier((block, before, after))
+    came_row = z_hi * 8 + (y - z_hi) % 4 * 2 + z_lo % 2
+    came_col = (2 * core + z_lo // 2) * 4 + x
+    block = block * mask_of(came_row, came_col).astype(BF)
     near = gather(block, "prow", ZLO)
     swapped = [send(part, swap) for part in (ancestor_inverse, before, after)]
     top, bottom = before[:half], after[half:]

time: 153 us -> 156 us (1.020)
  waiting for transfers between devices: 41.3 us -> 28.8 us
  blocking collectives: 16.8 us -> 27.3 us
  starting transfers between devices: 71.4 us -> 77.6 us
    all_to_all x2, blocking collectives: 16.8 us -> 27.3 us  [gather(): return lax.all_to_all(copies, axis, 0, 0, axis_index_groups=members)]
    ppermute x15, waiting for transfers between devices: 33.4 us -> 24.7 us  [send(): return lax.ppermute(block, BOTH, moves(to))]
    ppermute x15, starting transfers between devices: 58.4 us -> 63.9 us  [send(): return lax.ppermute(block, BOTH, moves(to))]
    all_to_all x2, waiting for transfers between devices: 7.93 us -> 4.04 us  [gather(): return lax.all_to_all(copies, axis, 0, 0, axis_index_groups=members)]
    unnamed x16 -> x18, local copies, waits for them, and re-layouts: 3.3 us -> 3.31 us
where the time goes in v5:
time: 156 us; the launch traced here: 155 us
  starting transfers between devices  77.6 us (50%)
  waiting for transfers between devices  28.8 us (18%)
  blocking collectives  27.3 us (18%)
  local copies, waits for them, and re-layouts  9.86 us (6%)
  Pallas kernels  6.3 us (4%)
  other arithmetic  4.34 us (3%)
    ppermute x15, starting transfers between devices, send(): return lax.ppermute(block, BOTH, moves(to))  63.9 us
    all_to_all x2, blocking collectives, gather(): return lax.all_to_all(copies, axis, 0, 0, axis_index_groups=members)  27.3 us
    ppermute x15, waiting for transfers between devices, send(): return lax.ppermute(block, BOTH, moves(to))  24.7 us
    all_to_all x2, starting transfers between devices, gather(): return lax.all_to_all(copies, axis, 0, 0, axis_index_groups=members)  13.7 us
    pallas_call x1, Pallas kernels, times(): pl.pallas_call(times_kernel, in_specs=[pl.BlockSpec(memory_space=pltpu.SM...  6.3 us
    all_to_all x2, waiting for transfers between devices, gather(): return lax.all_to_all(copies, axis, 0, 0, axis_index_groups=members)  4.04 us
    unnamed x18, local copies, waits for them, and re-layouts  3.31 us
  transfers between devices with their start and end apart: 17, of which 7 were waited for; matrix products, arithmetic and copies ran while one was open for 3% of the time, Pallas kernels for 0%

profile of v5, /device:TPU:1, one launch (start us, length us, event | category | flops | bytes accessed | tf_op | source)
XLA Modules:
  0.0 155.4 jit_solution(2021994964106297482)
XLA Ops:
  0.6 4.0 %collective-permute-start.2 = (bf16[512,1024]{1,0:T(8,128)(2,1)}, bf16[512,1024]{1,0:T(8,128)(2,1)S(1)}, u32[]{:S(2)}, u32[]{:S(2)}) collective-permute-start(bf16[512,1024]{1,0:T(8,128)(2,1)} %refs_0_.1), channel_id=1, source_target_pairs={{0,1},{1,2},{2,3},{3,0},{4,5},{5,6},{6,7},{7,4},{8,9},{9,10},{10,1... | collective-permute-start | bytes 3145736 | tf_op jit(solution)/shard_map/ppermute | solution.py:42
  4.6 3.2 %collective-permute-start.3 = (bf16[512,1024]{1,0:T(8,128)(2,1)}, bf16[512,1024]{1,0:T(8,128)(2,1)S(1)}, u32[]{:S(2)}, u32[]{:S(2)}) collective-permute-start(bf16[512,1024]{1,0:T(8,128)(2,1)} %refs_0_.1), channel_id=1, source_target_pairs={{0,3},{1,0},{2,1},{3,2},{4,7},{5,4},{6,5},{7,6},{8,11},{9,8},{10,9... | collective-permute-start | bytes 3145736 | tf_op jit(solution)/shard_map/ppermute | solution.py:42
  7.8 1.6 %collective-permute-start = (bf16[512,128]{1,0:T(8,128)(2,1)}, bf16[512,128]{1,0:T(8,128)(2,1)S(1)}, u32[]{:S(2)}, u32[]{:S(2)}) collective-permute-start(bf16[512,128]{1,0:T(8,128)(2,1)} %param.5), channel_id=1, source_target_pairs={{0,0},{1,1},{2,2},{3,3},{4,4},{5,5},{6,6},{7,7},{8,8},{9,9},{10,10... | collective-permute-start | bytes 393224 | tf_op jit(solution)/shard_map/ppermute | solution.py:42
  9.3 0.8 convert_bitcast_fusion
  10.1 0.0 collective-permute-done
  10.1 10.8 %collective-permute-start.1 = (bf16[512,128]{1,0:T(8,128)(2,1)S(1)}, bf16[512,128]{1,0:T(8,128)(2,1)S(1)}, u32[]{:S(2)}, u32[]{:S(2)}) collective-permute-start(bf16[512,128]{1,0:T(8,128)(2,1)S(1)} %collective-permute-done), channel_id=1, source_target_pairs={{0,0},{1,1},{2,2},{3,3},{4,64},{5,65},{6,66},{7,67},{8,16},{9,17},... | collective-permute-start | bytes 393224 | tf_op jit(solution)/shard_map/ppermute | solution.py:42
  20.9 0.1 broadcast_bitcast_fusion.2
  21.0 8.7 %collective-permute-done.1 = bf16[512,128]{1,0:T(8,128)(2,1)S(1)} collective-permute-done((bf16[512,128]{1,0:T(8,128)(2,1)S(1)}, bf16[512,128]{1,0:T(8,128)(2,1)S(1)}, u32[]{:S(2)}, u32[]{:S(2)}) %collective-permute-start.1) | collective-permute-done | bytes 131104 | tf_op jit(solution)/shard_map/ppermute | solution.py:42
  29.7 0.1 broadcast_multiply_fusion
  29.8 1.0 broadcast_in_dim.22
  30.9 7.1 %all-to-all-start = ((bf16[4,512,128]{2,1,0:T(8,128)(2,1)}), bf16[4,512,128]{2,1,0:T(8,128)(2,1)S(1)}, u32[]{:S(2)}, u32[]{:S(2)}) async-start(bf16[4,512,128]{2,1,0:T(8,128)(2,1)} %broadcast_in_dim.22), calls=%async_computation | async-start | bytes 1048576 | tf_op jit(solution)/shard_map/all_to_all | solution.py:84
  37.9 3.3 %collective-permute-start.4 = (bf16[512,1024]{1,0:T(8,128)(2,1)}, bf16[512,1024]{1,0:T(8,128)(2,1)S(1)}, u32[]{:S(2)}, u32[]{:S(2)}) collective-permute-start(bf16[512,1024]{1,0:T(8,128)(2,1)} %refs_0_.1), channel_id=1, source_target_pairs={{0,16},{1,17},{2,18},{3,19},{4,20},{5,21},{6,22},{7,23},{8,24},{9,... | collective-permute-start | bytes 3145736 | tf_op jit(solution)/shard_map/ppermute | solution.py:42
  41.2 1.9 %collective-permute-start.5 = (bf16[512,1024]{1,0:T(8,128)(2,1)S(1)}, bf16[512,1024]{1,0:T(8,128)(2,1)S(1)}, u32[]{:S(2)}, u32[]{:S(2)}) collective-permute-start(bf16[512,1024]{1,0:T(8,128)(2,1)S(1)} %collective-permute-done.2.refs_1_), channel_id=1, source_target_pairs={{0,16},{1,17},{2,18},{3,19},{4,20},{5,21},{6,22},{7,23},{8,24},{9,... | collective-permute-start | bytes 3145736 | tf_op jit(solution)/shard_map/ppermute | solution.py:42
  43.1 2.4 %collective-permute-start.6 = (bf16[512,1024]{1,0:T(8,128)(2,1)S(1)}, bf16[512,1024]{1,0:T(8,128)(2,1)}, u32[]{:S(2)}, u32[]{:S(2)}) collective-permute-start(bf16[512,1024]{1,0:T(8,128)(2,1)S(1)} %collective-permute-done.3.refs_2_), channel_id=1, source_target_pairs={{0,16},{1,17},{2,18},{3,19},{4,20},{5,21},{6,22},{7,23},{8,24},{9,... | collective-permute-start | bytes 3145736 | tf_op jit(solution)/shard_map/ppermute | solution.py:42
  45.6 0.9 slice.6
  46.4 0.9 slice.7
  47.3 1.0 copy-done.3
  48.3 1.0 copy-done.4
  49.3 2.6 %all-to-all-done = bf16[4,512,128]{2,1,0:T(8,128)(2,1)S(1)} async-done(((bf16[4,512,128]{2,1,0:T(8,128)(2,1)}), bf16[4,512,128]{2,1,0:T(8,128)(2,1)S(1)}, u32[]{:S(2)}, u32[]{:S(2)}) %all-to-all-start) | async-done | bytes 524320 | tf_op jit(solution)/shard_map/all_to_all | solution.py:84
  51.9 1.7 %broadcast_in_dim.23 = bf16[4,4,512,128]{3,2,1,0:T(8,128)(2,1)} broadcast(bf16[4,512,128]{2,1,0:T(8,128)(2,1)S(1)} %all-to-all-done), dimensions={1,2,3} | broadcast | bytes 2621440 | tf_op jit(solution)/shard_map/broadcast_in_dim | solution.py:83
  53.7 6.6 %all-to-all-start.1 = ((bf16[4,4,512,128]{3,2,1,0:T(8,128)(2,1)}), bf16[4,4,512,128]{3,2,1,0:T(8,128)(2,1)S(1)}, u32[]{:S(2)}, u32[]{:S(2)}) async-start(bf16[4,4,512,128]{3,2,1,0:T(8,128)(2,1)} %broadcast_in_dim.23), calls=%async_computation.1 | async-start | bytes 4194304 | tf_op jit(solution)/shard_map/all_to_all | solution.py:84
  60.3 2.9 %collective-permute-start.8 = (bf16[256,1024]{1,0:T(8,128)(2,1)}, bf16[256,1024]{1,0:T(8,128)(2,1)S(1)}, u32[]{:S(2)}, u32[]{:S(2)}) collective-permute-start(bf16[256,1024]{1,0:T(8,128)(2,1)} %slice.7), channel_id=1, source_target_pairs={{0,3},{1,0},{2,1},{3,2},{4,7},{5,4},{6,5},{7,6},{8,11},{9,8},{10,9... | collective-permute-start | bytes 1572872 | tf_op jit(solution)/shard_map/ppermute | solution.py:42
  63.1 2.4 %collective-permute-start.7 = (bf16[256,1024]{1,0:T(8,128)(2,1)}, bf16[256,1024]{1,0:T(8,128)(2,1)S(1)}, u32[]{:S(2)}, u32[]{:S(2)}) collective-permute-start(bf16[256,1024]{1,0:T(8,128)(2,1)} %slice.6), channel_id=1, source_target_pairs={{0,1},{1,2},{2,3},{3,0},{4,5},{5,6},{6,7},{7,4},{8,9},{9,10},{10,1... | collective-permute-start | bytes 1572872 | tf_op jit(solution)/shard_map/ppermute | solution.py:42
  65.6 9.4 %collective-permute-done.8.refs_4_ = bf16[256,1024]{1,0:T(8,128)(2,1)S(1)} collective-permute-done((bf16[256,1024]{1,0:T(8,128)(2,1)}, bf16[256,1024]{1,0:T(8,128)(2,1)S(1)}, u32[]{:S(2)}, u32[]{:S(2)}) %collective-permute-start.8) | collective-permute-done | bytes 524320 | tf_op jit(solution)/shard_map/ppermute | solution.py:42
  74.9 3.7 %collective-permute-start.10 = (bf16[256,1024]{1,0:T(8,128)(2,1)S(1)}, bf16[256,1024]{1,0:T(8,128)(2,1)}, u32[]{:S(2)}, u32[]{:S(2)}) collective-permute-start(bf16[256,1024]{1,0:T(8,128)(2,1)S(1)} %collective-permute-done.8.refs_4_), channel_id=1, source_target_pairs={{0,16},{1,17},{2,18},{3,19},{4,20},{5,21},{6,22},{7,23},{8,24},{9,... | collective-permute-start | bytes 1572872 | tf_op jit(solution)/shard_map/ppermute | solution.py:42
  78.6 4.1 %collective-permute-start.9 = (bf16[256,1024]{1,0:T(8,128)(2,1)S(1)}, bf16[256,1024]{1,0:T(8,128)(2,1)}, u32[]{:S(2)}, u32[]{:S(2)}) collective-permute-start(bf16[256,1024]{1,0:T(8,128)(2,1)S(1)} %collective-permute-done.7.refs_3_), channel_id=1, source_target_pairs={{0,16},{1,17},{2,18},{3,19},{4,20},{5,21},{6,22},{7,23},{8,24},{9,... | collective-permute-start | bytes 1572872 | tf_op jit(solution)/shard_map/ppermute | solution.py:42
  82.8 0.6 stack.31.order
  83.5 0.9 collective-permute-done.9.refs_8_
  84.4 1.4 all-to-all-done.1
  85.8 1.3 copy-done
  87.1 6.3 %shard_map.59 = bf16[4,512,128]{2,1,0:T(8,128)(2,1)} custom-call(s32[7]{0:T(128)} %stack.31.order, bf16[4,2,1024,128]{3,2,1,0:T(8,128)(2,1)} %bitcast.37, bf16[512,1024]{1,0:T(8,128)(2,1)} %refs_0_.1, bf16[512,1024]{1,0:T(8,128)(2,1)} %copy-done.1, bf16[512,1024]{1,0:T(8,128)(2,1)} %copy-done.2, bf16[256,1024]{1,0:T(8,128)(2,1)} %copy-done.6, ...), custom_call_target="tpu_custom_call" | custom-call | flops 2147483648 | bytes 9437184 | tf_op jit(solution)/shard_map/pallas_call | solution.py:122
  93.4 0.0 copy-start.8
  93.4 1.1 slice_bitcast_fusion.3
  94.5 0.0 copy-start.7
  94.5 8.0 %collective-permute-start.12 = (bf16[512,128]{1,0:T(8,128)(2,1)S(1)}, bf16[512,128]{1,0:T(8,128)(2,1)S(1)}, u32[]{:S(2)}, u32[]{:S(2)}) collective-permute-start(bf16[512,128]{1,0:T(8,128)(2,1)S(1)} %get-tuple-element.24), channel_id=1, source_target_pairs={{4,20},{5,21},{6,22},{7,23},{8,4},{9,5},{10,6},{11,7},{12,8},{13,9... | collective-permute-start | bytes 393224 | tf_op jit(solution)/shard_map/ppermute | solution.py:42
  102.5 1.9 %collective-permute-start.13 = (bf16[512,128]{1,0:T(8,128)(2,1)S(1)}, bf16[512,128]{1,0:T(8,128)(2,1)S(1)}, u32[]{:S(2)}, u32[]{:S(2)}) collective-permute-start(bf16[512,128]{1,0:T(8,128)(2,1)S(1)} %get-tuple-element.23), channel_id=1, source_target_pairs={{0,16},{1,17},{2,18},{3,19},{8,12},{9,13},{10,14},{11,15},{12,0},{... | collective-permute-start | bytes 393224 | tf_op jit(solution)/shard_map/ppermute | solution.py:42
  104.5 0.1 broadcast_bitcast_fusion
  104.5 6.3 %collective-permute-start.11 = (bf16[512,128]{1,0:T(8,128)(2,1)S(1)}, bf16[512,128]{1,0:T(8,128)(2,1)S(1)}, u32[]{:S(2)}, u32[]{:S(2)}) collective-permute-start(bf16[512,128]{1,0:T(8,128)(2,1)S(1)} %get-tuple-element.22), channel_id=1, source_target_pairs={{0,20},{1,21},{2,22},{3,23},{4,0},{5,1},{6,2},{7,3},{8,4},{9,5},{1... | collective-permute-start | bytes 393224 | tf_op jit(solution)/shard_map/ppermute | solution.py:42
  110.9 1.0 fusion
  111.9 7.5 %collective-permute-start.14 = (bf16[512,128]{1,0:T(8,128)(2,1)S(1)}, bf16[512,128]{1,0:T(8,128)(2,1)S(1)}, u32[]{:S(2)}, u32[]{:S(2)}) collective-permute-start(bf16[512,128]{1,0:T(8,128)(2,1)S(1)} %fusion), channel_id=1, source_target_pairs={{0,4},{1,5},{2,6},{3,7},{4,16},{5,17},{6,18},{7,19},{8,20},{9,21},... | collective-permute-start | bytes 393224 | tf_op jit(solution)/shard_map/ppermute | solution.py:42
  119.4 0.1 broadcast_bitcast_fusion.1
  119.5 2.1 %collective-permute-done.11 = bf16[512,128]{1,0:T(8,128)(2,1)S(1)} collective-permute-done((bf16[512,128]{1,0:T(8,128)(2,1)S(1)}, bf16[512,128]{1,0:T(8,128)(2,1)S(1)}, u32[]{:S(2)}, u32[]{:S(2)}) %collective-permute-start.11) | collective-permute-done | bytes 131104 | tf_op jit(solution)/shard_map/ppermute | solution.py:42
  121.5 3.7 %collective-permute-done.14 = bf16[512,128]{1,0:T(8,128)(2,1)S(1)} collective-permute-done((bf16[512,128]{1,0:T(8,128)(2,1)S(1)}, bf16[512,128]{1,0:T(8,128)(2,1)S(1)}, u32[]{:S(2)}, u32[]{:S(2)}) %collective-permute-start.14) | collective-permute-done | bytes 131104 | tf_op jit(solution)/shard_map/ppermute | solution.py:42
  125.3 1.8 %multiply_convert_fusion = (bf16[512,128]{1,0:T(8,128)(2,1)}, bf16[512,128]{1,0:T(8,128)(2,1)S(1)}) fusion(bf16[512,128]{1,0:T(8,128)(2,1)S(1)} %collective-permute-done.14, bf16[512,128]{1,0:T(8,128)(2,1)S(1)} %collective-permute-done.11, f32[512]{0:T(512)S(1)} %broadcast_bitcast_fusion, bf16[512,128]{1,0:T(8,128)(2,1)S(1)} %collective-permute-done.12, ...), kind=kLoop, calls=%fused_computation.4 | loop fusion | flops 720896 | bytes 1050627 | tf_op jit(solution)/shard_map/convert_element_type | solution.py:184
  127.0 0.3 convolution_convert_fusion
  127.4 14.4 %all_to_all.20 = bf16[8,128,128]{2,1,0:T(8,128)(2,1)S(1)} all-to-all(bf16[8,128,128]{2,1,0:T(8,128)(2,1)S(1)} %broadcast_in_dim.52), channel_id=1, replica_groups={{0,16,128,144,256,272,384,400},{32,48,160,176,288,304,416,432},{64,80,1..., dimensions={0} | all-to-all | bytes 524288 | tf_op jit(solution)/shard_map/all_to_all | solution.py:84
  141.9 12.9 %all_to_all.21 = bf16[4,128,128]{2,1,0:T(8,128)(2,1)S(1)} all-to-all(bf16[4,128,128]{2,1,0:T(8,128)(2,1)S(1)} %broadcast_in_dim.53), channel_id=1, replica_groups={{0,32,64,96},{16,48,80,112},{128,160,192,224},{144,176,208,240},{256,28..., dimensions={0} | all-to-all | bytes 262144 | tf_op jit(solution)/shard_map/all_to_all | solution.py:84
  154.8 0.6 add.127
  (26 shorter events, 0.2 us)
Async XLA Ops:
  0.6 29.1 %collective-permute-start.2 = (bf16[512,1024]{1,0:T(8,128)(2,1)}, bf16[512,1024]{1,0:T(8,128)(2,1)S(1)}, u32[]{:S(2)}, u32[]{:S(2)}) collective-permute-start(bf16[512,1024]{1,0:T(8,128)(2,1)} %refs_0_.1), channel_id=1, source_target_pairs={{0,1},{1,2},{2,3},{3,0},{4,5},{5,6},{6,7},{7,4},{8,9},{9,10},{10,1... | collective-permute-start | bytes 3145736 | tf_op jit(solution)/shard_map/ppermute | solution.py:42
  4.6 25.1 %collective-permute-start.3 = (bf16[512,1024]{1,0:T(8,128)(2,1)}, bf16[512,1024]{1,0:T(8,128)(2,1)S(1)}, u32[]{:S(2)}, u32[]{:S(2)}) collective-permute-start(bf16[512,1024]{1,0:T(8,128)(2,1)} %refs_0_.1), channel_id=1, source_target_pairs={{0,3},{1,0},{2,1},{3,2},{4,7},{5,4},{6,5},{7,6},{8,11},{9,8},{10,9... | collective-permute-start | bytes 3145736 | tf_op jit(solution)/shard_map/ppermute | solution.py:42
  7.8 2.3 %collective-permute-start = (bf16[512,128]{1,0:T(8,128)(2,1)}, bf16[512,128]{1,0:T(8,128)(2,1)S(1)}, u32[]{:S(2)}, u32[]{:S(2)}) collective-permute-start(bf16[512,128]{1,0:T(8,128)(2,1)} %param.5), channel_id=1, source_target_pairs={{0,0},{1,1},{2,2},{3,3},{4,4},{5,5},{6,6},{7,7},{8,8},{9,9},{10,10... | collective-permute-start | bytes 393224 | tf_op jit(solution)/shard_map/ppermute | solution.py:42
  10.1 19.6 %collective-permute-start.1 = (bf16[512,128]{1,0:T(8,128)(2,1)S(1)}, bf16[512,128]{1,0:T(8,128)(2,1)S(1)}, u32[]{:S(2)}, u32[]{:S(2)}) collective-permute-start(bf16[512,128]{1,0:T(8,128)(2,1)S(1)} %collective-permute-done), channel_id=1, source_target_pairs={{0,0},{1,1},{2,2},{3,3},{4,64},{5,65},{6,66},{7,67},{8,16},{9,17},... | collective-permute-start | bytes 393224 | tf_op jit(solution)/shard_map/ppermute | solution.py:42
  29.7 24.0 %copy-start.1 = (bf16[512,1024]{1,0:T(8,128)(2,1)}, bf16[512,1024]{1,0:T(8,128)(2,1)S(1)}, u32[]{:S(2)}) copy-start(bf16[512,1024]{1,0:T(8,128)(2,1)S(1)} %collective-permute-done.2.refs_1_) | copy-start | bytes 3145732
  29.7 24.0 %copy-start.2 = (bf16[512,1024]{1,0:T(8,128)(2,1)}, bf16[512,1024]{1,0:T(8,128)(2,1)S(1)}, u32[]{:S(2)}) copy-start(bf16[512,1024]{1,0:T(8,128)(2,1)S(1)} %collective-permute-done.3.refs_2_) | copy-start | bytes 3145732
  30.9 21.1 %all-to-all-start = ((bf16[4,512,128]{2,1,0:T(8,128)(2,1)}), bf16[4,512,128]{2,1,0:T(8,128)(2,1)S(1)}, u32[]{:S(2)}, u32[]{:S(2)}) async-start(bf16[4,512,128]{2,1,0:T(8,128)(2,1)} %broadcast_in_dim.22), calls=%async_computation | async-start | bytes 1048576 | tf_op jit(solution)/shard_map/all_to_all | solution.py:84
  37.9 9.4 %collective-permute-start.4 = (bf16[512,1024]{1,0:T(8,128)(2,1)}, bf16[512,1024]{1,0:T(8,128)(2,1)S(1)}, u32[]{:S(2)}, u32[]{:S(2)}) collective-permute-start(bf16[512,1024]{1,0:T(8,128)(2,1)} %refs_0_.1), channel_id=1, source_target_pairs={{0,16},{1,17},{2,18},{3,19},{4,20},{5,21},{6,22},{7,23},{8,24},{9,... | collective-permute-start | bytes 3145736 | tf_op jit(solution)/shard_map/ppermute | solution.py:42
  41.2 6.1 %collective-permute-start.5 = (bf16[512,1024]{1,0:T(8,128)(2,1)S(1)}, bf16[512,1024]{1,0:T(8,128)(2,1)S(1)}, u32[]{:S(2)}, u32[]{:S(2)}) collective-permute-start(bf16[512,1024]{1,0:T(8,128)(2,1)S(1)} %collective-permute-done.2.refs_1_), channel_id=1, source_target_pairs={{0,16},{1,17},{2,18},{3,19},{4,20},{5,21},{6,22},{7,23},{8,24},{9,... | collective-permute-start | bytes 3145736 | tf_op jit(solution)/shard_map/ppermute | solution.py:42
  43.1 6.2 %collective-permute-start.6 = (bf16[512,1024]{1,0:T(8,128)(2,1)S(1)}, bf16[512,1024]{1,0:T(8,128)(2,1)}, u32[]{:S(2)}, u32[]{:S(2)}) collective-permute-start(bf16[512,1024]{1,0:T(8,128)(2,1)S(1)} %collective-permute-done.3.refs_2_), channel_id=1, source_target_pairs={{0,16},{1,17},{2,18},{3,19},{4,20},{5,21},{6,22},{7,23},{8,24},{9,... | collective-permute-start | bytes 3145736 | tf_op jit(solution)/shard_map/ppermute | solution.py:42
  47.3 1.0 copy-start.3
  48.3 1.0 copy-start.4
  53.7 32.1 %all-to-all-start.1 = ((bf16[4,4,512,128]{3,2,1,0:T(8,128)(2,1)}), bf16[4,4,512,128]{3,2,1,0:T(8,128)(2,1)S(1)}, u32[]{:S(2)}, u32[]{:S(2)}) async-start(bf16[4,4,512,128]{3,2,1,0:T(8,128)(2,1)} %broadcast_in_dim.23), calls=%async_computation.1 | async-start | bytes 4194304 | tf_op jit(solution)/shard_map/all_to_all | solution.py:84
  60.3 14.6 %collective-permute-start.8 = (bf16[256,1024]{1,0:T(8,128)(2,1)}, bf16[256,1024]{1,0:T(8,128)(2,1)S(1)}, u32[]{:S(2)}, u32[]{:S(2)}) collective-permute-start(bf16[256,1024]{1,0:T(8,128)(2,1)} %slice.7), channel_id=1, source_target_pairs={{0,3},{1,0},{2,1},{3,2},{4,7},{5,4},{6,5},{7,6},{8,11},{9,8},{10,9... | collective-permute-start | bytes 1572872 | tf_op jit(solution)/shard_map/ppermute | solution.py:42
  63.1 15.5 %collective-permute-start.7 = (bf16[256,1024]{1,0:T(8,128)(2,1)}, bf16[256,1024]{1,0:T(8,128)(2,1)S(1)}, u32[]{:S(2)}, u32[]{:S(2)}) collective-permute-start(bf16[256,1024]{1,0:T(8,128)(2,1)} %slice.6), channel_id=1, source_target_pairs={{0,1},{1,2},{2,3},{3,0},{4,5},{5,6},{6,7},{7,4},{8,9},{9,10},{10,1... | collective-permute-start | bytes 1572872 | tf_op jit(solution)/shard_map/ppermute | solution.py:42
  74.9 10.9 %copy-start.5 = (bf16[256,1024]{1,0:T(8,128)(2,1)}, bf16[256,1024]{1,0:T(8,128)(2,1)S(1)}, u32[]{:S(2)}) copy-start(bf16[256,1024]{1,0:T(8,128)(2,1)S(1)} %collective-permute-done.8.refs_4_) | copy-start | bytes 1572868
  74.9 8.6 %collective-permute-start.10 = (bf16[256,1024]{1,0:T(8,128)(2,1)S(1)}, bf16[256,1024]{1,0:T(8,128)(2,1)}, u32[]{:S(2)}, u32[]{:S(2)}) collective-permute-start(bf16[256,1024]{1,0:T(8,128)(2,1)S(1)} %collective-permute-done.8.refs_4_), channel_id=1, source_target_pairs={{0,16},{1,17},{2,18},{3,19},{4,20},{5,21},{6,22},{7,23},{8,24},{9,... | collective-permute-start | bytes 1572872 | tf_op jit(solution)/shard_map/ppermute | solution.py:42
  78.6 7.2 %copy-start.6 = (bf16[256,1024]{1,0:T(8,128)(2,1)}, bf16[256,1024]{1,0:T(8,128)(2,1)S(1)}, u32[]{:S(2)}) copy-start(bf16[256,1024]{1,0:T(8,128)(2,1)S(1)} %collective-permute-done.7.refs_3_) | copy-start | bytes 1572868
  78.6 5.7 %collective-permute-start.9 = (bf16[256,1024]{1,0:T(8,128)(2,1)S(1)}, bf16[256,1024]{1,0:T(8,128)(2,1)}, u32[]{:S(2)}, u32[]{:S(2)}) collective-permute-start(bf16[256,1024]{1,0:T(8,128)(2,1)S(1)} %collective-permute-done.7.refs_3_), channel_id=1, source_target_pairs={{0,16},{1,17},{2,18},{3,19},{4,20},{5,21},{6,22},{7,23},{8,24},{9,... | collective-permute-start | bytes 1572872 | tf_op jit(solution)/shard_map/ppermute | solution.py:42
  85.8 1.3 copy-start
  93.4 33.6 %copy-start.8 = (bf16[512,128]{1,0:T(8,128)(2,1)S(1)}, bf16[512,128]{1,0:T(8,128)(2,1)}, u32[]{:S(2)}) copy-start(bf16[512,128]{1,0:T(8,128)(2,1)} %param.5) | copy-start | bytes 393220
  94.5 60.3 %copy-start.7 = (f32[128,128]{1,0:T(8,128)S(1)}, f32[128,128]{1,0:T(8,128)}, u32[]{:S(2)}) copy-start(f32[128,128]{1,0:T(8,128)} %param.7) | copy-start | bytes 196612
  94.5 16.4 %collective-permute-start.12 = (bf16[512,128]{1,0:T(8,128)(2,1)S(1)}, bf16[512,128]{1,0:T(8,128)(2,1)S(1)}, u32[]{:S(2)}, u32[]{:S(2)}) collective-permute-start(bf16[512,128]{1,0:T(8,128)(2,1)S(1)} %get-tuple-element.24), channel_id=1, source_target_pairs={{4,20},{5,21},{6,22},{7,23},{8,4},{9,5},{10,6},{11,7},{12,8},{13,9... | collective-permute-start | bytes 393224 | tf_op jit(solution)/shard_map/ppermute | solution.py:42
  102.5 8.3 %collective-permute-start.13 = (bf16[512,128]{1,0:T(8,128)(2,1)S(1)}, bf16[512,128]{1,0:T(8,128)(2,1)S(1)}, u32[]{:S(2)}, u32[]{:S(2)}) collective-permute-start(bf16[512,128]{1,0:T(8,128)(2,1)S(1)} %get-tuple-element.23), channel_id=1, source_target_pairs={{0,16},{1,17},{2,18},{3,19},{8,12},{9,13},{10,14},{11,15},{12,0},{... | collective-permute-start | bytes 393224 | tf_op jit(solution)/shard_map/ppermute | solution.py:42
  104.5 17.0 %collective-permute-start.11 = (bf16[512,128]{1,0:T(8,128)(2,1)S(1)}, bf16[512,128]{1,0:T(8,128)(2,1)S(1)}, u32[]{:S(2)}, u32[]{:S(2)}) collective-permute-start(bf16[512,128]{1,0:T(8,128)(2,1)S(1)} %get-tuple-element.22), channel_id=1, source_target_pairs={{0,20},{1,21},{2,22},{3,23},{4,0},{5,1},{6,2},{7,3},{8,4},{9,5},{1... | collective-permute-start | bytes 393224 | tf_op jit(solution)/shard_map/ppermute | solution.py:42
  111.9 13.4 %collective-permute-start.14 = (bf16[512,128]{1,0:T(8,128)(2,1)S(1)}, bf16[512,128]{1,0:T(8,128)(2,1)S(1)}, u32[]{:S(2)}, u32[]{:S(2)}) collective-permute-start(bf16[512,128]{1,0:T(8,128)(2,1)S(1)} %fusion), channel_id=1, source_target_pairs={{0,4},{1,5},{2,6},{3,7},{4,16},{5,17},{6,18},{7,19},{8,20},{9,21},... | collective-permute-start | bytes 393224 | tf_op jit(solution)/shard_map/ppermute | solution.py:42
